TPU v7x, 128 devices: a whole 4x4x4 slice. The times are simulated.
128 devices in a mesh: dp: 8 (over x, core), vocab: 4 (over z), width: 4 (over y).
Axes of the slice: x: 4, y: 4, z: 4, core: 2. Of those that a mesh axis runs over, the one named last changes fastest.
Arguments:
- tokens: bfloat16 [32768, 8192], P(('dp', 'vocab'), 'width'), may hold values from -300 to 300
- table: float32 [12288, 8192], P(('dp', 'vocab'), 'width'), may hold values from -6 to 6
- moment_one: float32 [12288, 8192], P(('dp', 'vocab'), 'width'), may hold values from -4 to 4
- moment_two: float32 [12288, 8192], P(('dp', 'vocab'), 'width'), may hold values from 0.01 to 1
- block_ids: int32 [8], replicated, may hold values from 0 to 95, as said below
- targets: int32 [32768], P(('dp', 'vocab')), may hold values from 0 to 1023
Outputs:
- new_table: float32 [12288, 8192], P(('dp', 'vocab'), 'width')
- new_moment_one: float32 [12288, 8192], P(('dp', 'vocab'), 'width')
- new_moment_two: float32 [12288, 8192], P(('dp', 'vocab'), 'width')
- token_grads: bfloat16 [32768, 8192], P(('dp', 'vocab'), 'width')
Inputs may be any that keep to these rules, and one draw needn't show every extreme that they name: `block_ids`: the shortlist's blocks are distinct; no owner (rows of table of one device along dp+vocab, 3 blocks) holds more than 3 of them, and one owner holds exactly 3.
All inputs are finite; a program needn't handle non-finite values.
Results may differ from a plain program's by a relative error of at most 0.009.
The roundings to bfloat16 on the way count: a program that leaves them out, or rounds other values in their place, can miss the bound.
Values may be sent and summed in bfloat16 or wider, within the bound.
A program may use at most 192 MiB of HBM per device.

v0:
```python
import math

import jax
import jax.numpy as jnp
from jax import lax
from jax.sharding import PartitionSpec as P

D = 8192
BLOCK = 128


beta_one = 0.9
beta_two = 0.95
learn_rate = 0.01
decay_rate = 0.1
epsilon = 1e-08


def adamw_rows(weights, first, second, grads):
    first_new = beta_one * first + (1.0 - beta_one) * grads
    second_new = beta_two * second + (1.0 - beta_two) * grads * grads
    correct_one = 1.0 - beta_one**10
    correct_two = 1.0 - beta_two**10
    update = (
        first_new / correct_one / (jnp.sqrt(second_new / correct_two) + epsilon)
        + decay_rate * weights
    )
    return (weights - learn_rate * update, first_new, second_new)


def place_block(blocks, update, where_block, owned_flag):
    current = lax.dynamic_index_in_dim(blocks, where_block, 0, keepdims=False)
    chosen = jnp.where(owned_flag, update, current)
    return lax.dynamic_update_index_in_dim(blocks, chosen, where_block, 0)


def body(tokens, table, moment_one, moment_two, block_ids, targets):
    my_owner = lax.axis_index(("dp", "vocab"))
    width_cols = table.shape[1]
    own_blocks = table.shape[0] // BLOCK
    block_count = block_ids.shape[0]
    short_count = block_count * BLOCK
    owner_of = block_ids // own_blocks
    local_block = block_ids % own_blocks
    is_mine = owner_of == my_owner
    weight_blocks = table.reshape(own_blocks, BLOCK, width_cols)
    first_blocks = moment_one.reshape(own_blocks, BLOCK, width_cols)
    second_blocks = moment_two.reshape(own_blocks, BLOCK, width_cols)
    picked = weight_blocks[local_block]
    masked = (
        jnp.where(is_mine[:, None, None], picked, 0.0)
        .astype(jnp.bfloat16)
        .reshape(short_count, width_cols)
    )
    short_rows = lax.psum(masked, ("dp", "vocab")).astype(jnp.float32).astype(jnp.bfloat16)
    logit_scale = 1.0 / math.sqrt(D)
    partial_logits = lax.dot_general(
        tokens, short_rows, (((1,), (1,)), ((), ())), preferred_element_type=jnp.float32
    )
    logits = lax.psum(partial_logits, "width") * logit_scale
    row_max = jnp.max(logits, axis=1, keepdims=True)
    exponent = jnp.exp(logits - row_max)
    probability = exponent / jnp.sum(exponent, axis=1, keepdims=True)
    columns = jnp.arange(short_count, dtype=jnp.int32)
    onehot = (targets[:, None] == columns[None, :]).astype(jnp.float32)
    dlogits = (probability - onehot).astype(jnp.bfloat16)
    token_grads = (
        jnp.dot(dlogits, short_rows, preferred_element_type=jnp.float32) * logit_scale
    ).astype(jnp.bfloat16)
    partial_grad = lax.optimization_barrier(
        (
            lax.dot_general(
                dlogits, tokens, (((0,), (0,)), ((), ())), preferred_element_type=jnp.float32
            )
            * logit_scale
        ).astype(jnp.bfloat16)
    )
    row_grad = lax.psum(
        partial_grad.astype(jnp.float32).astype(jnp.bfloat16), ("dp", "vocab")
    ).astype(jnp.float32)
    grad_blocks = row_grad.reshape(block_count, BLOCK, width_cols)
    new_w, new_m, new_v = adamw_rows(
        picked, first_blocks[local_block], second_blocks[local_block], grad_blocks
    )
    for position in range(block_count):
        weight_blocks = place_block(
            weight_blocks, new_w[position], local_block[position], is_mine[position]
        )
        first_blocks = place_block(
            first_blocks, new_m[position], local_block[position], is_mine[position]
        )
        second_blocks = place_block(
            second_blocks, new_v[position], local_block[position], is_mine[position]
        )
    new_table = weight_blocks.reshape(table.shape)
    new_first = first_blocks.reshape(table.shape)
    new_second = second_blocks.reshape(table.shape)
    return (new_table, new_first, new_second, token_grads)


def solution(mesh):
    placed = (
        P(("dp", "vocab"), "width"),
        P(("dp", "vocab"), "width"),
        P(("dp", "vocab"), "width"),
        P(("dp", "vocab"), "width"),
        P(),
        P(("dp", "vocab")),
    )
    return jax.shard_map(
        body,
        mesh=mesh,
        in_specs=placed,
        out_specs=(
            P(("dp", "vocab"), "width"),
            P(("dp", "vocab"), "width"),
            P(("dp", "vocab"), "width"),
            P(("dp", "vocab"), "width"),
        ),
        check_vma=False,
    )
```

profile of v0, /device:TPU:1, one launch (start us, length us, event | category | flops | bytes accessed | tf_op | source)
XLA Modules:
  0.0 429.0 jit_solution(6139778458034804837)
XLA Ops:
  7.2 0.0 all-reduce.4.cloned.1.call-start
  7.2 0.0 copy-start.8
  7.2 4.1 copy.40
  11.3 0.0 copy-done.8
  11.3 0.2 copy.41
  11.5 1.7 copy-done.9
  13.2 1.7 copy.42
  14.8 0.0 copy-done.12
  14.9 0.1 broadcast_bitcast_fusion
  15.0 6.2 %gather_fusion = f32[8,128,2048]{2,1,0:T(8,128)} fusion(f32[3,128,2048]{2,1,0:T(8,128)} %bitcast.41, s32[1024]{0:T(1024)S(1)} %pad_clamp_fusion), kind=kCustom, calls=%fused_computation | custom fusion | bytes 16777248 | tf_op jit(solution)/shard_map/gather | solution.py:49
  21.2 5.9 %fusion.2 = bf16[1024,2048]{1,0:T(8,128)(2,1)} fusion(f32[8,128,2048]{2,1,0:T(8,128)} %gather_fusion, pred[1024]{0:T(1024)(128)(4,1)S(1)} %broadcast_bitcast_fusion), kind=kLoop, calls=%fused_computation.8 | loop fusion | flops 2097152 | bytes 12583936 | tf_op jit(solution)/shard_map/convert_element_type | solution.py:52
  27.1 0.0 all-reduce.4.cloned.1.call-update
  27.1 0.0 all-reduce.6.cloned.1.call-start
  27.2 115.1 %all-reduce.4.cloned.1.call-done = bf16[1024,2048]{1,0:T(8,128)(2,1)} async-done(((bf16[1024,2048]{1,0:T(8,128)(2,1)}), bf16[1024,2048]{1,0:T(8,128)(2,1)}) %all-reduce.4.cloned.1.call-update) | async-done | bytes 4194320 | tf_op jit(solution)/shard_map/psum | solution.py:55
  142.3 10.0 %convolution_bitcast_fusion = f32[1024,1024]{0,1:T(8,128)} fusion(bf16[1024,2048]{1,0:T(8,128)(2,1)} %all-reduce.4.cloned.1.call-done, bf16[1024,2048]{1,0:T(8,128)(2,1)} %param.6), kind=kOutput, calls=%fused_computation.17 | convolution fusion | flops 4294967296 | bytes 12582912 | tf_op jit(solution)/shard_map/dot_general | solution.py:57
  152.3 0.0 all-reduce.6.cloned.1.call-update
  152.3 0.0 copy-start.11
  152.3 0.2 all-reduce.8.cloned.1.call-start
  152.5 92.3 %all-reduce.6.cloned.1.call-done = f32[1024,1024]{0,1:T(8,128)} async-done(((f32[1024,1024]{0,1:T(8,128)}), f32[1024,1024]{0,1:T(8,128)}) %all-reduce.6.cloned.1.call-update) | async-done | bytes 4194320 | tf_op jit(solution)/shard_map/psum | solution.py:60
  244.8 2.7 multiply_reduce_fusion
  247.5 0.7 copy-done.7
  248.3 0.7 fusion.3
  249.0 0.5 copy-done.10
  249.5 6.4 %multiply_convert_fusion.1 = bf16[1024,2048]{1,0:T(8,128)(2,1)} fusion(bf16[1024,2048]{1,0:T(8,128)(2,1)S(1)} %copy-done.10, f32[1024,1024]{0,1:T(8,128)S(1)} %copy-done.7, s32[1024]{0:T(1024)S(1)} %copy-done.11, f32[1024]{0:T(1024)S(1)} %fusion.3, f32[1024]{0:T(1024)S(1)} %multiply_reduce_fusion), kind=kOutput, calls=%fused_computation.11 | convolution fusion | flops 4306501632 | bytes 12595200 | tf_op jit(solution)/shard_map/dot_general | solution.py:72
  255.9 0.0 all-reduce.8.cloned.1.call-update
  256.0 0.7 fusion.32
  267.0 6.3 %gather_fusion.2 = f32[8,128,2048]{2,1,0:T(8,128)} fusion(f32[3,128,2048]{2,1,0:T(8,128)} %bitcast.38, s32[1024]{0:T(1024)S(1)} %pad_clamp_fusion), kind=kCustom, calls=%fused_computation.2 | custom fusion | bytes 16777248 | tf_op jit(solution)/shard_map/gather | solution.py:83
  273.3 4.3 %gather_fusion.1 = f32[8,128,2048]{2,1,0:T(8,128)} fusion(f32[3,128,2048]{2,1,0:T(8,128)S(1)} %bitcast.35, s32[1024]{0:T(1024)S(1)} %pad_clamp_fusion), kind=kCustom, calls=%fused_computation.1 | custom fusion | bytes 16777248 | tf_op jit(solution)/shard_map/gather | solution.py:83
  282.7 0.7 fusion.31
  283.4 10.6 %multiply_convert_fusion = bf16[1024,2048]{1,0:T(8,128)(2,1)} fusion(bf16[1024,2048]{1,0:T(8,128)(2,1)} %all-reduce.4.cloned.1.call-done, f32[1024,1024]{0,1:T(8,128)} %all-reduce.6.cloned.1.call-done, s32[1024]{0:T(1024)S(1)} %copy-done.11, f32[1024]{0:T(1024)S(1)} %fusion.3, f32[1024]{0:T(1024)S(1)} %multiply_reduce_fusion), kind=kOutput, calls=%fused_computation.9 | convolution fusion | flops 4306501632 | bytes 12595200 | tf_op jit(solution)/shard_map/dot_general | solution.py:68
  294.0 73.8 %all-reduce.8.cloned.1.call-done = bf16[8,128,2048]{2,1,0:T(8,128)(2,1)} async-done(((bf16[8,128,2048]{2,1,0:T(8,128)(2,1)}), bf16[8,128,2048]{2,1,0:T(8,128)(2,1)}) %all-reduce.8.cloned.1.call-update) | async-done | bytes 4194320 | tf_op jit(solution)/shard_map/psum | solution.py:78
  367.8 19.9 %multiply_subtract_fusion = (f32[8,128,2048]{2,1,0:T(8,128)}, f32[8,128,2048]{2,1,0:T(8,128)}, f32[8,128,2048]{2,1,0:T(8,128)}) fusion(f32[8,128,2048]{2,1,0:T(8,128)} %gather_fusion, bf16[8,128,2048]{2,1,0:T(8,128)(2,1)} %all-reduce.8.cloned.1.call-done, f32[8,128,2048]{2,1,0:T(8,128)} %gather_fusion.1, f32[8,128,2048]{2,1,0:T(8,128)} %gather_fusion.2), kind=kLoop, calls=%fused_computation.10 | loop fusion | flops 33554432 | bytes 54525952 | tf_op jit(solution)/shard_map/sub | solution.py:28
  387.7 3.5 fusion.27
  391.2 4.0 fusion.11
  395.2 3.3 fusion.10
  398.5 0.0 copy-done.3
  398.5 1.0 fusion.26
  399.5 0.0 copy-start.6
  399.5 2.4 fusion.18
  401.9 0.0 slice-start
  401.9 2.9 fusion.9
  404.8 2.0 fusion.17
  406.8 0.0 slice-start.1
  406.9 1.0 fusion.25
  407.8 1.1 fusion.8
  409.0 0.9 fusion.24
  409.9 0.9 fusion.16
  410.8 0.8 fusion.7
  411.5 0.8 fusion.15
  412.3 0.7 fusion.23
  413.1 0.9 fusion.6
  413.9 0.9 fusion.22
  414.8 0.9 fusion.14
  415.7 0.8 fusion.5
  416.5 0.8 fusion.13
  417.4 0.8 fusion.4
  418.2 0.0 copy-start.2
  418.2 0.9 fusion.12
  419.1 0.0 copy-start
  419.1 0.8 fusion.21
  420.0 0.9 fusion.20
  420.8 0.0 copy-start.4
  420.8 0.1 copy-done
  420.9 1.6 copy-done.4
  (18 shorter events, 0.1 us)
Async XLA Ops:
  7.2 135.1 %all-reduce.4.cloned.1.call-start = ((), (), s32[]{:S(2)}) async-start(), calls=%async_computation | async-start | bytes 8388608 | tf_op jit(solution)/shard_map/psum | solution.py:55
  7.2 4.1 copy-start.8
  11.3 1.9 copy-start.9
  13.2 1.7 copy-start.12
  27.1 217.7 %all-reduce.6.cloned.1.call-start = ((), (), s32[]{:S(2)}) async-start(), calls=%async_computation.1 | async-start | bytes 8388608 | tf_op jit(solution)/shard_map/psum | solution.py:60
  152.3 96.7 %copy-start.11 = (s32[1024]{0:T(1024)S(1)}, s32[1024]{0:T(1024)}, u32[]{:S(2)}) copy-start(s32[1024]{0:T(1024)} %param.11) | copy-start | bytes 12292
  152.3 215.5 %all-reduce.8.cloned.1.call-start = ((), (), s32[]{:S(2)}) async-start(), calls=%async_computation.2 | async-start | bytes 8388608 | tf_op jit(solution)/shard_map/psum | solution.py:78
  244.8 3.4 copy-start.7
  244.8 4.7 %copy-start.10 = (bf16[1024,2048]{1,0:T(8,128)(2,1)S(1)}, bf16[1024,2048]{1,0:T(8,128)(2,1)}, u32[]{:S(2)}) copy-start(bf16[1024,2048]{1,0:T(8,128)(2,1)} %param.6) | copy-start | bytes 12582916
  387.7 10.8 %copy-start.5 = (f32[8,128,2048]{2,1,0:T(8,128)S(1)}, f32[8,128,2048]{2,1,0:T(8,128)}, u32[]{:S(2)}) copy-start(f32[8,128,2048]{2,1,0:T(8,128)} %get-tuple-element.4) | copy-start | bytes 25165828
  391.2 7.3 %copy-start.3 = (f32[3,128,2048]{2,1,0:T(8,128)S(1)}, f32[3,128,2048]{2,1,0:T(8,128)}, u32[]{:S(2)}) copy-start(f32[3,128,2048]{2,1,0:T(8,128)} %fusion.27) | copy-start | bytes 9437188
  398.5 3.4 copy-start.1
  399.5 8.3 %copy-start.6 = (f32[8,128,2048]{2,1,0:T(8,128)S(1)}, f32[8,128,2048]{2,1,0:T(8,128)}, u32[]{:S(2)}) copy-start(f32[8,128,2048]{2,1,0:T(8,128)} %get-tuple-element.6) | copy-start | bytes 25165828
  401.9 8.0 %slice-start = ((s8[8388608]{0:T(1024)(128)(4,1)}), s8[4194304]{0:T(1024)(128)(4,1)S(1)}, s32[]{:S(2)}) async-start(s8[8388608]{0:T(1024)(128)(4,1)} %bitcast.44), calls=%async_computation.3 | async-start | bytes 8388608
  406.8 3.0 slice-start.1
  418.2 2.6 copy-start.2
  419.1 1.8 copy-start
  420.8 1.7 copy-start.4
Sparse Core Ops, SparseCore 0:
  27.2 114.9 all-reduce.3
  152.4 92.3 all-reduce.5
  256.1 111.6 all-reduce.7
where the time goes:
time: 430 us; the launch traced here: 429 us
  waiting for transfers between devices  281 us (65%)
  other arithmetic  62.2 us (14%)
  between operations  29.5 us (7%)
  local copies, waits for them, and re-layouts  28.8 us (7%)
  matrix products  27 us (6%)
    psum x1, waiting for transfers between devices, body(): lax.psum(masked, ('dp', 'vocab')).astype(jnp.float32).astype(jnp.bfloat16)  115 us
    psum x1, waiting for transfers between devices, body(): logits = lax.psum(partial_logits, 'width') * logit_scale  92.3 us
    psum x1, waiting for transfers between devices, body(): lax.psum(partial_grad.astype(jnp.float32).astype(jnp.bfloat16), ('dp', 'v...  73.8 us
    dynamic_update_slice x23, other arithmetic, place_block(): return lax.dynamic_update_index_in_dim(blocks, chosen, where_block, 0)  32.9 us
    sub x1, other arithmetic, adamw_rows(): return (weights - learn_rate * update, first_new, second_new)  19.9 us
    unnamed x33, local copies, waits for them, and re-layouts  10.6 us
    dot_general x1, matrix products, body(): jnp.dot(dlogits, short_rows, preferred_element_type=jnp.float32)  10.6 us
    dot_general x1, matrix products, body(): lax.dot_general(tokens, short_rows, (((1,), (1,)), ((), ())), preferred_e...  10 us
  transfers between devices with their start and end apart: 3, of which 3 were waited for; matrix products, arithmetic and copies ran while one was open for 5% of the time, Pallas kernels for 0%

commit v1 on v0

v1 whole, which is shorter than its diff:
```python
import functools
import math

import jax
import jax.numpy as jnp
from jax import lax
from jax.experimental import pallas as pl
from jax.experimental.pallas import tpu as pltpu
from jax.sharding import PartitionSpec as P

D = 8192
BLOCK = 128
SCALE = 1.0 / math.sqrt(D)
MESH = pl.DeviceIdType.MESH
BF16 = jnp.bfloat16
F32 = jnp.float32

beta_one = 0.9
beta_two = 0.95
learn_rate = 0.01
decay_rate = 0.1
epsilon = 1e-08

N_SEM = 111


def adamw_rows(weights, first, second, grads):
    first_new = beta_one * first + (1.0 - beta_one) * grads
    second_new = beta_two * second + (1.0 - beta_two) * grads * grads
    correct_one = 1.0 - beta_one**10
    correct_two = 1.0 - beta_two**10
    update = (
        first_new / correct_one / (jnp.sqrt(second_new / correct_two) + epsilon)
        + decay_rate * weights
    )
    return (weights - learn_rate * update, first_new, second_new)


def mod4(v):
    return lax.rem(v + 4, 4)


def rows_at(start, size):
    return pl.ds(pl.multiple_of(start, size), size)


def comm_kernel(
    ids, tokens, table, targets,
    rows_out, dl_out, grad_out,
    tok, tab, tab6, tab_send, rows, part, dl, dl_t, acc, g_send, g_recv, grad,
    sums, half_sums, rs1, rs2, rt1, rt2, y1, y2,
    send_sem, recv_sem, local_sem,
):
    dp = lax.axis_index("dp")
    z = lax.axis_index("vocab")
    y = lax.axis_index("width")
    x = dp // 2
    c = lax.rem(dp, 2)
    rank = {"x": x, "z": z, "y": y}
    pending = []

    def near(axis, step):
        if axis == "x":
            return (mod4(x + step) * 2 + c, z, y)
        if axis == "z":
            return (dp, mod4(z + step), y)
        return (dp, z, mod4(y + step))

    peer = (x * 2 + (1 - c), z, y)

    def send(src, dst, device):
        i = len(pending)
        copy = pltpu.make_async_remote_copy(
            src_ref=src, dst_ref=dst, send_sem=send_sem.at[i], recv_sem=recv_sem.at[i],
            device_id=device, device_id_type=MESH,
        )
        copy.start()
        pending.append(copy)
        return copy

    def load(src, dst, i):
        copy = pltpu.make_async_copy(src, dst, local_sem.at[i])
        copy.start()
        return copy

    tab_copy = load(table, tab, 0)
    tok_copy = load(tokens, tok, 1)

    barrier = pltpu.get_barrier_semaphore()
    partners = [near(a, s) for a in "xzy" for s in (1, -1)] + [peer]
    for device in partners:
        pl.semaphore_signal(barrier, inc=1, device_id=device, device_id_type=MESH)
    pl.semaphore_wait(barrier, len(partners))

    class Scatter:
        def __init__(self, axis, piece, first, second):
            self.axis, self.piece, self.first, self.second = axis, piece, first, second
            self.r = rank[axis]

        def far(self):
            far = mod4(self.r + 2)
            self.far_up = send(self.piece(far, 0), self.first.at[0], near(self.axis, 1))
            self.far_down = send(self.piece(far, 1), self.first.at[1], near(self.axis, -1))

        def direct(self):
            up, down = mod4(self.r + 1), mod4(self.r - 1)
            self.direct_up = send(self.piece(up, 1), self.second.at[0, 1], near(self.axis, 1))
            self.direct_down = send(self.piece(down, 0), self.second.at[1, 0], near(self.axis, -1))

        def relay(self):
            up, down = mod4(self.r + 1), mod4(self.r - 1)
            self.far_up.wait_recv()
            ref = self.piece(up, 0)
            ref[...] = (ref[...].astype(F32) + self.first[0].astype(F32)).astype(ref.dtype)
            self.relay_up = send(ref, self.second.at[0, 0], near(self.axis, 1))
            self.far_down.wait_recv()
            ref = self.piece(down, 1)
            ref[...] = (ref[...].astype(F32) + self.first[1].astype(F32)).astype(ref.dtype)
            self.relay_down = send(ref, self.second.at[1, 1], near(self.axis, -1))

        def finish(self, h):
            if h == 0:
                self.relay_up.wait_recv()
                self.direct_down.wait_recv()
            else:
                self.direct_up.wait_recv()
                self.relay_down.wait_recv()
            return (
                self.piece(self.r, h)[...].astype(F32)
                + self.second[0, h].astype(F32)
                + self.second[1, h].astype(F32)
            )

    class Gather:
        def __init__(self, axis, place):
            self.axis, self.place = axis, place
            self.r = rank[axis]

        def start(self):
            own = self.place(self.r, None)
            self.up = send(own, own, near(self.axis, 1))
            self.down = send(own, own, near(self.axis, -1))

        def relay(self):
            self.up.wait_recv()
            ref = self.place(mod4(self.r - 1), 0)
            self.relay_up = send(ref, ref, near(self.axis, 1))
            self.down.wait_recv()
            ref = self.place(mod4(self.r + 1), 1)
            self.relay_down = send(ref, ref, near(self.axis, -1))

        def finish(self):
            self.relay_up.wait_recv()
            self.relay_down.wait_recv()

    def plane_all_reduce(n, result):
        axes = (("x", "z"), ("z", "x"))
        outer = []
        for half, (a, b) in enumerate(axes):
            def piece(p, h, half=half):
                return sums.at[n, p, rows_at(half * 512 + h * 256, 256), :]
            outer.append(Scatter(a, piece, rs1.at[n, half], rs2.at[n, half]))
        for s in outer:
            s.far()
        for s in outer:
            s.direct()
        for s in outer:
            s.relay()
        inner = []
        for half, (a, b) in enumerate(axes):
            for h in range(2):
                half_sums[n, half, h * 256:(h + 1) * 256, :] = outer[half].finish(h).astype(BF16)
            def piece(p, h, half=half):
                return half_sums.at[n, half, rows_at(p * 128 + h * 64, 64), :]
            s = Scatter(b, piece, rt1.at[n, half], rt2.at[n, half])
            s.far()
            s.direct()
            inner.append(s)
        for s in inner:
            s.relay()
        gathers = []
        for half, (a, b) in enumerate(axes):
            chunk = c * 4 + rank[a]
            for h in range(2):
                result[chunk, rows_at(half * 512 + rank[b] * 128 + h * 64, 64), :] = (
                    inner[half].finish(h).astype(BF16)
                )
            def place(p, h, half=half, chunk=chunk):
                if h is None:
                    return result.at[chunk, rows_at(half * 512 + p * 128, 128), :]
                return result.at[chunk, rows_at(half * 512 + p * 128 + h * 64, 64), :]
            s = Gather(b, place)
            s.start()
            gathers.append(s)
        for s in gathers:
            s.relay()
        outer = []
        across = []

        def hand_over(p, half):
            ref = result.at[c * 4 + p, rows_at(half * 512, 512), :]
            across.append(send(ref, ref, peer))

        for half, (a, b) in enumerate(axes):
            gathers[half].finish()
            def place(p, h, half=half):
                if h is None:
                    return result.at[c * 4 + p, rows_at(half * 512, 512), :]
                return result.at[c * 4 + p, rows_at(half * 512 + h * 256, 256), :]
            s = Gather(a, place)
            s.start()
            outer.append(s)
            hand_over(rank[a], half)
        for half, s in enumerate(outer):
            s.relay()
            hand_over(mod4(s.r - 1), half)
            hand_over(mod4(s.r + 1), half)
        for half, s in enumerate(outer):
            s.finish()
            hand_over(mod4(s.r + 2), half)
        for copy in across:
            copy.wait_recv()

    tab_copy.wait()
    for k in range(4):
        cols = pl.ds(pl.multiple_of((1 - c) * 1024 + k * 256, 256), 256)
        for j in range(3):
            tab_send[j, k] = tab[j * BLOCK:(j + 1) * BLOCK, cols].astype(BF16)
    table_half = send(tab_send, tab6.at[pl.ds(c * 3, 3)], peer)
    for k in range(4):
        cols = pl.ds(pl.multiple_of(c * 1024 + k * 256, 256), 256)
        for j in range(3):
            tab6[c * 3 + j, k] = tab[j * BLOCK:(j + 1) * BLOCK, cols].astype(BF16)
    table_half.wait_recv()
    for b in range(8):
        block = ids[b]
        owner = block // 3
        owner_dp = owner // 4
        here = jnp.logical_and(lax.rem(owner, 4) == z, owner_dp // 2 == x)
        slot = lax.rem(owner_dp, 2) * 3 + lax.rem(block, 3)
        for k in range(4):
            sums[0, k, b * BLOCK:(b + 1) * BLOCK, :] = jnp.where(
                here, tab6[slot, k].astype(F32), 0.0
            ).astype(BF16)
    plane_all_reduce(0, rows)
    rows_copy = load(rows, rows_out, 2)

    tok_copy.wait()

    def logits_of(p):
        @pl.loop(0, 4)
        def _(n):
            total = jnp.zeros((256, 256), F32)
            for k in range(8):
                total += lax.dot_general(
                    tok[rows_at(p * 256, 256), k * 256:(k + 1) * 256],
                    rows[k, rows_at(n * 256, 256), :],
                    (((1,), (1,)), ((), ())),
                    preferred_element_type=F32,
                )
            part[rows_at(p * 256, 256), pl.ds(pl.multiple_of(n * 256, 256), 256)] = total

    def part_piece(p, h):
        return part.at[rows_at(p * 256 + h * 128, 128), :]

    s = Scatter("y", part_piece, y1, y2)
    logits_of(mod4(y + 2))
    s.far()
    logits_of(mod4(y + 1))
    logits_of(mod4(y - 1))
    s.direct()
    logits_of(y)
    s.relay()

    for h in range(2):
        logits = s.finish(h) * SCALE
        exponent = jnp.exp(logits - jnp.max(logits, axis=1, keepdims=True))
        probability = exponent * (1.0 / jnp.sum(exponent, axis=1, keepdims=True))
        line = targets[pl.ds(y * 2 + h, 1), :].astype(F32)
        column = jnp.transpose(jnp.broadcast_to(line, (128, 128)))[:, :1]
        place = lax.broadcasted_iota(jnp.int32, (128, 1024), 1).astype(F32)
        onehot = jnp.where(column == place, 1.0, 0.0)
        dl[rows_at(y * 256 + h * 128, 128), :] = (probability - onehot).astype(BF16)

    def dl_place(p, h):
        if h is None:
            return dl.at[rows_at(p * 256, 256), :]
        return dl.at[rows_at(p * 256 + h * 128, 128), :]

    g = Gather("y", dl_place)
    g.start()

    def turn(p):
        dl_t[p] = jnp.transpose(dl[rows_at(p * 256, 256), :])

    def product(p, k, n):
        return jnp.dot(
            dl_t[p, rows_at(n * 512, 512), :],
            tok[rows_at(p * 256, 256), pl.ds(pl.multiple_of(k * 256, 256), 256)],
            preferred_element_type=F32,
        )

    def each_tile(f):
        @pl.loop(0, 8)
        def _(k):
            @pl.loop(0, 2)
            def _(n):
                f(k, n)

    turn(y)

    def first(k, n):
        acc[k, rows_at(n * 512, 512), :] = product(y, k, n)

    each_tile(first)
    g.relay()
    up, down, far = mod4(y + 1), mod4(y - 1), mod4(y + 2)
    turn(up)
    turn(down)

    def second(k, n):
        acc[k, rows_at(n * 512, 512), :] += product(up, k, n) + product(down, k, n)

    each_tile(second)
    g.finish()
    dl_copy = load(dl, dl_out, 3)
    turn(far)

    crossing = []
    for q in range(4):
        k = (1 - c) * 4 + q
        @pl.loop(0, 2)
        def _(n):
            here = rows_at(n * 512, 512)
            g_send[q, here, :] = ((acc[k, here, :] + product(far, k, n)) * SCALE).astype(BF16)
        crossing.append(send(g_send.at[q], g_recv.at[q], peer))
    for q in range(4):
        k = c * 4 + q
        crossing[q].wait_recv()
        @pl.loop(0, 2)
        def _(n):
            here = rows_at(n * 512, 512)
            total = (acc[k, here, :] + product(far, k, n)) * SCALE
            sums[1, q, here, :] = (total + g_recv[q, here, :].astype(F32)).astype(BF16)
    plane_all_reduce(1, grad)
    grad_copy = load(grad, grad_out, 4)

    assert len(pending) == N_SEM, len(pending)
    for copy in pending:
        copy.wait_send()
    rows_copy.wait()
    dl_copy.wait()
    grad_copy.wait()


def communicate(ids, tokens, table, targets):
    vmem = pltpu.VMEM
    return pl.pallas_call(
        comm_kernel,
        out_shape=(
            jax.ShapeDtypeStruct((8, 1024, 256), BF16),
            jax.ShapeDtypeStruct((1024, 1024), BF16),
            jax.ShapeDtypeStruct((8, 1024, 256), BF16),
        ),
        in_specs=[
            pl.BlockSpec(memory_space=pltpu.SMEM),
            pl.BlockSpec(memory_space=pl.ANY),
            pl.BlockSpec(memory_space=pl.ANY),
            pl.BlockSpec(memory_space=pltpu.VMEM),
        ],
        out_specs=(pl.BlockSpec(memory_space=pl.ANY),) * 3,
        scratch_shapes=[
            vmem((1024, 2048), BF16),
            vmem((384, 2048), F32),
            vmem((6, 4, 128, 256), BF16),
            vmem((3, 4, 128, 256), BF16),
            vmem((8, 1024, 256), BF16),
            vmem((1024, 1024), F32),
            vmem((1024, 1024), BF16),
            vmem((4, 1024, 256), BF16),
            vmem((8, 1024, 256), F32),
            vmem((4, 1024, 256), BF16),
            vmem((4, 1024, 256), BF16),
            vmem((8, 1024, 256), BF16),
            vmem((2, 4, 1024, 256), BF16),
            vmem((2, 2, 512, 256), BF16),
            vmem((2, 2, 2, 256, 256), BF16),
            vmem((2, 2, 2, 2, 256, 256), BF16),
            vmem((2, 2, 2, 64, 256), BF16),
            vmem((2, 2, 2, 2, 64, 256), BF16),
            vmem((2, 128, 1024), F32),
            vmem((2, 2, 128, 1024), F32),
            pltpu.SemaphoreType.DMA((N_SEM,)),
            pltpu.SemaphoreType.DMA((N_SEM,)),
            pltpu.SemaphoreType.DMA((5,)),
        ],
        compiler_params=pltpu.CompilerParams(
            collective_id=0, has_side_effects=True, vmem_limit_bytes=60 * 2**20
        ),
    )(ids, tokens, table, targets)


def update_kernel(
    where_ref, dl, rows, g0, g1, g2, w, m, v, w_out, m_out, v_out, tok_out
):
    tok_out[...] = (
        jnp.dot(dl[...], rows[0], preferred_element_type=F32) * SCALE
    ).astype(BF16)
    for j, g in enumerate((g0, g1, g2)):
        here = slice(j * BLOCK, (j + 1) * BLOCK)
        listed = where_ref[3 + j] > 0
        old = (w[here, :], m[here, :], v[here, :])
        new = adamw_rows(*old, g[0].astype(F32))
        w_out[here, :] = jnp.where(listed, new[0], old[0])
        m_out[here, :] = jnp.where(listed, new[1], old[1])
        v_out[here, :] = jnp.where(listed, new[2], old[2])


def update(where, dl, rows, grad, table, moment_one, moment_two):
    wide = pl.BlockSpec((384, 256), lambda k, s: (0, k))
    grad_spec = [
        pl.BlockSpec((1, BLOCK, 256), lambda k, s, j=j: (k, s[j], 0)) for j in range(3)
    ]
    return pl.pallas_call(
        update_kernel,
        grid_spec=pltpu.PrefetchScalarGridSpec(
            num_scalar_prefetch=1,
            grid=(8,),
            in_specs=[
                pl.BlockSpec((1024, 1024), lambda k, s: (0, 0)),
                pl.BlockSpec((1, 1024, 256), lambda k, s: (k, 0, 0)),
                *grad_spec,
                wide, wide, wide,
            ],
            out_specs=[wide, wide, wide, pl.BlockSpec((1024, 256), lambda k, s: (0, k))],
        ),
        out_shape=[jax.ShapeDtypeStruct((384, 2048), F32)] * 3
        + [jax.ShapeDtypeStruct((1024, 2048), BF16)],
        compiler_params=pltpu.CompilerParams(vmem_limit_bytes=48 * 2**20),
    )(where, dl, rows, grad, grad, grad, table, moment_one, moment_two)


def body(tokens, table, moment_one, moment_two, block_ids, targets):
    owner = lax.axis_index(("dp", "vocab"))
    mine = owner * 3 + jnp.arange(3, dtype=jnp.int32)
    match = block_ids[None, :] == mine[:, None]
    listed = jnp.any(match, axis=1).astype(jnp.int32)
    place = jnp.argmax(match, axis=1).astype(jnp.int32)
    where = jnp.concatenate([place, listed])
    rows, dl, grad = communicate(block_ids, tokens, table, targets.reshape(8, 128))
    return tuple(update(where, dl, rows, grad, table, moment_one, moment_two))


def solution(mesh):
    wide = P(("dp", "vocab"), "width")
    return jax.shard_map(
        body,
        mesh=mesh,
        in_specs=(wide, wide, wide, wide, P(), P(("dp", "vocab"))),
        out_specs=(wide, wide, wide, wide),
        check_vma=False,
    )
```

time: 430 us -> 177 us (0.41)
  waiting for transfers between devices: 281 us -> 0 us
  Pallas kernels: 0 us -> 172 us
  other arithmetic: 62.2 us -> 2.28 us
  between operations: 29.5 us -> 0.67 us
  local copies, waits for them, and re-layouts: 28.8 us -> 1.59 us
  matrix products: 27 us -> 0 us
    psum x3 -> x0, waiting for transfers between devices: 281 us -> none  [the longest x1 115 us: body(): lax.psum(masked, ('dp', 'vocab')).astype(jnp.float32).astype(jnp.bfloat16)]
    pallas_call x0 -> x2, Pallas kernels: none -> 172 us  [the longest x1 158 us: communicate(): pl.pallas_call(comm_kernel, out_shape=(jax.ShapeDtypeStruct((8, 1024, 256...]
    dynamic_update_slice x23 -> x0, other arithmetic: 32.9 us -> none  [place_block(): return lax.dynamic_update_index_in_dim(blocks, chosen, where_block, 0)]
    dot_general x3 -> x0, matrix products: 27 us -> none  [the longest x1 10.6 us: body(): jnp.dot(dlogits, short_rows, preferred_element_type=jnp.float32)]
    sub x1 -> x0, other arithmetic: 19.9 us -> none  [adamw_rows(): return (weights - learn_rate * update, first_new, second_new)]
    gather x3 -> x0, local copies, waits for them, and re-layouts: 16.8 us -> none  [the longest x1 6.27 us: body(): second_blocks[local_block]]
    unnamed x33 -> x4, local copies, waits for them, and re-layouts: 10.6 us -> 1.59 us
    convert_element_type x1, other arithmetic: 5.93 us -> 0.01 us  [body(): listed = jnp.any(match, axis=1).astype(jnp.int32)]
  transfers between devices with their start and end apart: 3 -> 0, of which waited for: 3 -> 0; matrix products, arithmetic and copies ran while one was open for 5% -> 0% of each run, Pallas kernels for 0% -> 0%
where the time goes in v1:
time: 177 us
  Pallas kernels  172 us (97%)
  other arithmetic  2.28 us (1%)
    pallas_call x1, Pallas kernels, communicate(): pl.pallas_call(comm_kernel, out_shape=(jax.ShapeDtypeStruct((8, 1024, 256...  158 us
    pallas_call x1, Pallas kernels, update(): pl.pallas_call(update_kernel, grid_spec=pltpu.PrefetchScalarGridSpec(num_...  14.1 us

profile of v1, /device:TPU:1, one launch (start us, length us, event | category | flops | bytes accessed | tf_op | source)
XLA Modules:
  0.0 176.6 jit_solution(15765147175459726056)
XLA Ops:
  0.6 0.8 compare_reduce_fusion
  1.5 1.4 compare_reduce_fusion.1
  2.9 0.1 pad_add_fusion.where_ref
  2.9 0.0 copy-start
  2.9 157.9 %shard_map.93 = (bf16[8,1024,256]{2,1,0:T(8,128)(2,1)}, bf16[1024,1024]{1,0:T(8,128)(2,1)}, bf16[8,1024,256]{2,1,0:T(8,128)(2,1)}) custom-call(s32[8]{0:T(128)} %ids.1, bf16[1024,2048]{1,0:T(8,128)(2,1)} %tokens.1, f32[384,2048]{1,0:T(8,128)} %w.1, s32[8,128]{1,0:T(8,128)} %bitcast.1), custom_call_target="tpu_custom_call" | custom-call | tf_op jit(solution)/shard_map/pallas_call | solution.py:358
  160.9 0.0 copy-done
  160.9 0.0 copy-start.1
  160.9 1.6 copy-done.1
  162.5 14.1 %shard_map.94 = (f32[384,2048]{1,0:T(8,128)}, f32[384,2048]{1,0:T(8,128)}, f32[384,2048]{1,0:T(8,128)}, bf16[1024,2048]{1,0:T(8,128)(2,1)}) custom-call(s32[6]{0:T(128)S(1)} %pad_add_fusion.where_ref, bf16[1024,1024]{1,0:T(8,128)(2,1)S(1)} %copy-done.1, bf16[8,1024,256]{2,1,0:T(8,128)(2,1)} %get-tuple-element.10.rows, ...), custom_call_target="tpu_custom_call" | custom-call | tf_op jit(solution)/shard_map/pallas_call | solution.py:424
  (2 shorter events, 0.0 us)
Async XLA Ops:
  2.9 157.9 %copy-start = (f32[384,2048]{1,0:T(8,128)S(1)}, f32[384,2048]{1,0:T(8,128)}, u32[]{:S(2)}) copy-start(f32[384,2048]{1,0:T(8,128)} %w.1) | copy-start | bytes 9437188
  160.9 1.6 copy-start.1

commit v2 on v1

--- a/solution.py
+++ b/solution.py
@@ -14,6 +14,9 @@
 MESH = pl.DeviceIdType.MESH
 BF16 = jnp.bfloat16
 F32 = jnp.float32
+WIRE = jnp.int16
+STEPS = 32700.0
+LOG_STEP = 256.0
 
 beta_one = 0.9
 beta_two = 0.95
@@ -21,7 +24,7 @@
 decay_rate = 0.1
 epsilon = 1e-08
 
-N_SEM = 111
+N_SEM = 289
 
 
 def adamw_rows(weights, first, second, grads):
@@ -47,8 +50,8 @@
 def comm_kernel(
     ids, tokens, table, targets,
     rows_out, dl_out, grad_out,
-    tok, tab, tab6, tab_send, rows, part, dl, dl_t, acc, g_send, g_recv, grad,
-    sums, half_sums, rs1, rs2, rt1, rt2, y1, y2,
+    tok, tab, tab6, tab_send, rows, part, wire, dl, dl_t, acc, g_send, g_recv, grad,
+    sums, half_sums, rs1, rs2, rt1, rt2, y1, y2, column,
     send_sem, recv_sem, local_sem,
 ):
     dp = lax.axis_index("dp")
@@ -96,35 +99,50 @@
         def __init__(self, axis, piece, first, second):
             self.axis, self.piece, self.first, self.second = axis, piece, first, second
             self.r = rank[axis]
+            self.above, self.below = mod4(self.r + 1), mod4(self.r - 1)
+            self.up, self.down = near(axis, 1), near(axis, -1)
 
         def far(self):
             far = mod4(self.r + 2)
-            self.far_up = send(self.piece(far, 0), self.first.at[0], near(self.axis, 1))
-            self.far_down = send(self.piece(far, 1), self.first.at[1], near(self.axis, -1))
+            self.far_up = send(self.piece(far, 0), self.first.at[0], self.up)
+            self.far_down = send(self.piece(far, 1), self.first.at[1], self.down)
+
+        def direct_up(self):
+            self.own_up = send(self.piece(self.above, 1), self.second.at[0, 1], self.up)
+
+        def direct_down(self):
+            self.own_down = send(self.piece(self.below, 0), self.second.at[1, 0], self.down)
 
         def direct(self):
-            up, down = mod4(self.r + 1), mod4(self.r - 1)
-            self.direct_up = send(self.piece(up, 1), self.second.at[0, 1], near(self.axis, 1))
-            self.direct_down = send(self.piece(down, 0), self.second.at[1, 0], near(self.axis, -1))
+            self.direct_up()
+            self.direct_down()
+
+        def add(self, p, h, more):
+            ref = self.piece(p, h)
+            ref[...] = (ref[...].astype(F32) + more[...].astype(F32)).astype(ref.dtype)
+            return ref
+
+        def relay_up(self):
+            self.far_up.wait_recv()
+            ref = self.add(self.above, 0, self.first.at[0])
+            self.sum_up = send(ref, self.second.at[0, 0], self.up)
+
+        def relay_down(self):
+            self.far_down.wait_recv()
+            ref = self.add(self.below, 1, self.first.at[1])
+            self.sum_down = send(ref, self.second.at[1, 1], self.down)
 
         def relay(self):
-            up, down = mod4(self.r + 1), mod4(self.r - 1)
-            self.far_up.wait_recv()
-            ref = self.piece(up, 0)
-            ref[...] = (ref[...].astype(F32) + self.first[0].astype(F32)).astype(ref.dtype)
-            self.relay_up = send(ref, self.second.at[0, 0], near(self.axis, 1))
-            self.far_down.wait_recv()
-            ref = self.piece(down, 1)
-            ref[...] = (ref[...].astype(F32) + self.first[1].astype(F32)).astype(ref.dtype)
-            self.relay_down = send(ref, self.second.at[1, 1], near(self.axis, -1))
-
-        def finish(self, h):
-            if h == 0:
-                self.relay_up.wait_recv()
-                self.direct_down.wait_recv()
-            else:
-                self.direct_up.wait_recv()
-                self.relay_down.wait_recv()
+            self.relay_up()
+            self.relay_down()
+
+        def arrived(self):
+            self.sum_up.wait_recv()
+            self.own_down.wait_recv()
+            self.own_up.wait_recv()
+            self.sum_down.wait_recv()
+
+        def total(self, h):
             return (
                 self.piece(self.r, h)[...].astype(F32)
                 + self.second[0, h].astype(F32)
@@ -141,83 +159,150 @@
             self.up = send(own, own, near(self.axis, 1))
             self.down = send(own, own, near(self.axis, -1))
 
-        def relay(self):
+        def relay_up(self):
             self.up.wait_recv()
             ref = self.place(mod4(self.r - 1), 0)
-            self.relay_up = send(ref, ref, near(self.axis, 1))
+            self.next_up = send(ref, ref, near(self.axis, 1))
+
+        def relay_down(self):
             self.down.wait_recv()
             ref = self.place(mod4(self.r + 1), 1)
-            self.relay_down = send(ref, ref, near(self.axis, -1))
+            self.next_down = send(ref, ref, near(self.axis, -1))
+
+        def relay(self):
+            self.relay_up()
+            self.relay_down()
 
         def finish(self):
-            self.relay_up.wait_recv()
-            self.relay_down.wait_recv()
+            self.next_up.wait_recv()
+            self.next_down.wait_recv()
 
     def plane_all_reduce(n, result):
+        halves = range(2)
         axes = (("x", "z"), ("z", "x"))
-        outer = []
-        for half, (a, b) in enumerate(axes):
-            def piece(p, h, half=half):
-                return sums.at[n, p, rows_at(half * 512 + h * 256, 256), :]
-            outer.append(Scatter(a, piece, rs1.at[n, half], rs2.at[n, half]))
-        for s in outer:
-            s.far()
-        for s in outer:
-            s.direct()
-        for s in outer:
-            s.relay()
+
+        def blocks_of(half):
+            r = rank[axes[half][1]]
+            return [mod4(r + 2), mod4(r + 1), mod4(r - 1), r]
+
+        outer = [[], []]
         inner = []
         for half, (a, b) in enumerate(axes):
-            for h in range(2):
-                half_sums[n, half, h * 256:(h + 1) * 256, :] = outer[half].finish(h).astype(BF16)
+            for i, block in enumerate(blocks_of(half)):
+                def piece(p, h, half=half, block=block):
+                    return sums.at[n, p, rows_at(half * 512 + block * 128 + h * 64, 64), :]
+                outer[half].append(Scatter(a, piece, rs1.at[n, half, i], rs2.at[n, half, i]))
             def piece(p, h, half=half):
                 return half_sums.at[n, half, rows_at(p * 128 + h * 64, 64), :]
-            s = Scatter(b, piece, rt1.at[n, half], rt2.at[n, half])
-            s.far()
-            s.direct()
-            inner.append(s)
-        for s in inner:
-            s.relay()
-        gathers = []
+            inner.append(Scatter(b, piece, rt1.at[n, half], rt2.at[n, half]))
+
+        def finish(half, i):
+            outer[half][i].arrived()
+            block = blocks_of(half)[i]
+            for h in range(2):
+                half_sums[n, half, rows_at(block * 128 + h * 64, 64), :] = (
+                    outer[half][i].total(h).astype(BF16)
+                )
+
+        for i in range(4):
+            for half in halves:
+                outer[half][i].far()
+            if i >= 1:
+                for half in halves:
+                    outer[half][i - 1].direct()
+        for half in halves:
+            outer[half][3].direct()
+        for half in halves:
+            outer[half][0].relay()
+        for half in halves:
+            outer[half][1].relay()
+        for half in halves:
+            finish(half, 0)
+            inner[half].far()
+        for half in halves:
+            outer[half][2].relay()
+        for half in halves:
+            finish(half, 1)
+            inner[half].direct_up()
+        for half in halves:
+            outer[half][3].relay()
+        for half in halves:
+            inner[half].relay_up()
+            finish(half, 2)
+            inner[half].direct_down()
+            inner[half].relay_down()
+        for half in halves:
+            finish(half, 3)
+
+        across = []
+        inner_gather = []
+        outer_gather = [[], []]
+
+        def hand_over(half, p, block):
+            ref = result.at[c * 4 + p, rows_at(half * 512 + block * 128, 128), :]
+            across.append(send(ref, ref, peer))
+
+        def spread(half, block):
+            a = axes[half][0]
+            def place(p, h):
+                if h is None:
+                    return result.at[c * 4 + p, rows_at(half * 512 + block * 128, 128), :]
+                return result.at[c * 4 + p, rows_at(half * 512 + block * 128 + h * 64, 64), :]
+            g = Gather(a, place)
+            g.start()
+            outer_gather[half].append((g, block))
+            hand_over(half, rank[a], block)
+
         for half, (a, b) in enumerate(axes):
             chunk = c * 4 + rank[a]
+            inner[half].arrived()
             for h in range(2):
                 result[chunk, rows_at(half * 512 + rank[b] * 128 + h * 64, 64), :] = (
-                    inner[half].finish(h).astype(BF16)
+                    inner[half].total(h).astype(BF16)
                 )
             def place(p, h, half=half, chunk=chunk):
                 if h is None:
                     return result.at[chunk, rows_at(half * 512 + p * 128, 128), :]
                 return result.at[chunk, rows_at(half * 512 + p * 128 + h * 64, 64), :]
-            s = Gather(b, place)
-            s.start()
-            gathers.append(s)
-        for s in gathers:
-            s.relay()
-        outer = []
-        across = []
-
-        def hand_over(p, half):
-            ref = result.at[c * 4 + p, rows_at(half * 512, 512), :]
-            across.append(send(ref, ref, peer))
-
-        for half, (a, b) in enumerate(axes):
-            gathers[half].finish()
-            def place(p, h, half=half):
-                if h is None:
-                    return result.at[c * 4 + p, rows_at(half * 512, 512), :]
-                return result.at[c * 4 + p, rows_at(half * 512 + h * 256, 256), :]
-            s = Gather(a, place)
-            s.start()
-            outer.append(s)
-            hand_over(rank[a], half)
-        for half, s in enumerate(outer):
-            s.relay()
-            hand_over(mod4(s.r - 1), half)
-            hand_over(mod4(s.r + 1), half)
-        for half, s in enumerate(outer):
-            s.finish()
-            hand_over(mod4(s.r + 2), half)
+            g = Gather(b, place)
+            g.start()
+            inner_gather.append(g)
+            spread(half, rank[b])
+
+        def spread_relay(half, i):
+            g, block = outer_gather[half][i]
+            g.relay_up()
+            hand_over(half, mod4(g.r - 1), block)
+            g.relay_down()
+            hand_over(half, mod4(g.r + 1), block)
+
+        def spread_finish(half, i):
+            g, block = outer_gather[half][i]
+            g.finish()
+            hand_over(half, mod4(g.r + 2), block)
+
+        for half in halves:
+            g = inner_gather[half]
+            g.relay_up()
+            spread(half, mod4(g.r - 1))
+            g.relay_down()
+            spread(half, mod4(g.r + 1))
+        for half in halves:
+            spread_relay(half, 0)
+        for half in halves:
+            g = inner_gather[half]
+            g.finish()
+            spread(half, mod4(g.r + 2))
+        for half in halves:
+            spread_relay(half, 1)
+            spread_relay(half, 2)
+        for half in halves:
+            spread_finish(half, 0)
+        for half in halves:
+            spread_relay(half, 3)
+        for half in halves:
+            for i in range(1, 4):
+                spread_finish(half, i)
         for copy in across:
             copy.wait_recv()
 
@@ -258,37 +343,83 @@
                     (((1,), (1,)), ((), ())),
                     preferred_element_type=F32,
                 )
-            part[rows_at(p * 256, 256), pl.ds(pl.multiple_of(n * 256, 256), 256)] = total
-
-    def part_piece(p, h):
-        return part.at[rows_at(p * 256 + h * 128, 128), :]
-
-    s = Scatter("y", part_piece, y1, y2)
+            part[rows_at(p * 256, 256), pl.ds(pl.multiple_of(n * 256, 256), 256)] = total * SCALE
+
+    def encode(start):
+        @pl.loop(0, 4)
+        def _(t):
+            some = rows_at(start + t * 16, 16)
+            value = part[some, :]
+            peak = jnp.max(jnp.abs(value), axis=1, keepdims=True)
+            power = jnp.ceil(jnp.log(jnp.maximum(peak, 1e-18)) * LOG_STEP)
+            steps = value * (jnp.exp(power * (-1.0 / LOG_STEP)) * STEPS)
+            wire[some, :1024] = jnp.round(steps).astype(jnp.int32).astype(WIRE)
+            wire[some, 1024:] = jnp.broadcast_to(power, (16, 128)).astype(jnp.int32).astype(WIRE)
+
+    def decode(message):
+        power = message[:, 1024:].astype(F32)[:, :1]
+        return message[:, :1024].astype(F32) * (jnp.exp(power * (1.0 / LOG_STEP)) * (1.0 / STEPS))
+
+    class LogitScatter(Scatter):
+        def __init__(self, u):
+            self.u = u
+            super().__init__("y", self.encoded, y1.at[u], y2.at[u])
+
+        def start(self, p, h):
+            return pl.multiple_of(p * 256 + self.u * 128 + h * 64, 64)
+
+        def encoded(self, p, h):
+            encode(self.start(p, h))
+            return wire.at[rows_at(self.start(p, h), 64), :]
+
+        def add(self, p, h, more):
+            @pl.loop(0, 4)
+            def _(t):
+                part[rows_at(self.start(p, h) + t * 16, 16), :] += decode(more[rows_at(t * 16, 16), :])
+            return self.encoded(p, h)
+
+    parts = [LogitScatter(u) for u in range(2)]
     logits_of(mod4(y + 2))
-    s.far()
+    parts[0].far()
+    parts[1].far()
     logits_of(mod4(y + 1))
+    parts[0].direct_up()
     logits_of(mod4(y - 1))
-    s.direct()
+    parts[0].direct_down()
+    parts[0].relay()
+    parts[1].direct()
     logits_of(y)
-    s.relay()
-
-    for h in range(2):
-        logits = s.finish(h) * SCALE
-        exponent = jnp.exp(logits - jnp.max(logits, axis=1, keepdims=True))
-        probability = exponent * (1.0 / jnp.sum(exponent, axis=1, keepdims=True))
-        line = targets[pl.ds(y * 2 + h, 1), :].astype(F32)
-        column = jnp.transpose(jnp.broadcast_to(line, (128, 128)))[:, :1]
-        place = lax.broadcasted_iota(jnp.int32, (128, 1024), 1).astype(F32)
-        onehot = jnp.where(column == place, 1.0, 0.0)
-        dl[rows_at(y * 256 + h * 128, 128), :] = (probability - onehot).astype(BF16)
-
-    def dl_place(p, h):
-        if h is None:
-            return dl.at[rows_at(p * 256, 256), :]
-        return dl.at[rows_at(p * 256 + h * 128, 128), :]
-
-    g = Gather("y", dl_place)
-    g.start()
+    parts[1].relay()
+
+    gathers = []
+    for u in range(2):
+        parts[u].arrived()
+        line = targets[pl.ds(y * 2 + u, 1), :].astype(F32)
+        column[...] = jnp.transpose(jnp.broadcast_to(line, (128, 128)))
+
+        @pl.loop(0, 4)
+        def _(t):
+            h, some = t // 2, rows_at(lax.rem(t, 2) * 32, 32)
+            logits = (
+                part[rows_at(y * 256 + u * 128 + t * 32, 32), :]
+                + decode(y2[u, 0, h, some, :])
+                + decode(y2[u, 1, h, some, :])
+            )
+            exponent = jnp.exp(logits - jnp.max(logits, axis=1, keepdims=True))
+            probability = exponent * (1.0 / jnp.sum(exponent, axis=1, keepdims=True))
+            place = lax.broadcasted_iota(jnp.int32, (32, 1024), 1).astype(F32)
+            onehot = jnp.where(column[rows_at(t * 32, 32), :1] == place, 1.0, 0.0)
+            dl[rows_at(y * 256 + u * 128 + t * 32, 32), :] = (probability - onehot).astype(BF16)
+
+        def dl_place(p, h, u=u):
+            if h is None:
+                return dl.at[rows_at(p * 256 + u * 128, 128), :]
+            return dl.at[rows_at(p * 256 + u * 128 + h * 64, 64), :]
+
+        g = Gather("y", dl_place)
+        g.start()
+        gathers.append(g)
+    gathers[0].relay()
 
     def turn(p):
         dl_t[p] = jnp.transpose(dl[rows_at(p * 256, 256), :])
@@ -313,7 +444,7 @@
         acc[k, rows_at(n * 512, 512), :] = product(y, k, n)
 
     each_tile(first)
-    g.relay()
+    gathers[1].relay()
     up, down, far = mod4(y + 1), mod4(y - 1), mod4(y + 2)
     turn(up)
     turn(down)
@@ -322,7 +453,8 @@
         acc[k, rows_at(n * 512, 512), :] += product(up, k, n) + product(down, k, n)
 
     each_tile(second)
-    g.finish()
+    for g in gathers:
+        g.finish()
     dl_copy = load(dl, dl_out, 3)
     turn(far)
 
@@ -376,6 +508,7 @@
             vmem((3, 4, 128, 256), BF16),
             vmem((8, 1024, 256), BF16),
             vmem((1024, 1024), F32),
+            vmem((1024, 1152), WIRE),
             vmem((1024, 1024), BF16),
             vmem((4, 1024, 256), BF16),
             vmem((8, 1024, 256), F32),
@@ -384,12 +517,13 @@
             vmem((8, 1024, 256), BF16),
             vmem((2, 4, 1024, 256), BF16),
             vmem((2, 2, 512, 256), BF16),
-            vmem((2, 2, 2, 256, 256), BF16),
-            vmem((2, 2, 2, 2, 256, 256), BF16),
+            vmem((2, 2, 4, 2, 64, 256), BF16),
+            vmem((2, 2, 4, 2, 2, 64, 256), BF16),
             vmem((2, 2, 2, 64, 256), BF16),
             vmem((2, 2, 2, 2, 64, 256), BF16),
-            vmem((2, 128, 1024), F32),
-            vmem((2, 2, 128, 1024), F32),
+            vmem((2, 2, 64, 1152), WIRE),
+            vmem((2, 2, 2, 64, 1152), WIRE),
+            vmem((128, 128), F32),
             pltpu.SemaphoreType.DMA((N_SEM,)),
             pltpu.SemaphoreType.DMA((N_SEM,)),
             pltpu.SemaphoreType.DMA((5,)),
@@ -400,6 +534,15 @@
     )(ids, tokens, table, targets)
 
 
+def listed_at(where, j):
+    place, listed = 0, 0
+    for b in range(8):
+        same = where[b] == where[8] + j
+        place = jnp.where(same, b, place)
+        listed = jnp.where(same, 1, listed)
+    return place, listed
+
+
 def update_kernel(
     where_ref, dl, rows, g0, g1, g2, w, m, v, w_out, m_out, v_out, tok_out
 ):
@@ -408,7 +551,7 @@
     ).astype(BF16)
     for j, g in enumerate((g0, g1, g2)):
         here = slice(j * BLOCK, (j + 1) * BLOCK)
-        listed = where_ref[3 + j] > 0
+        listed = listed_at(where_ref, j)[1] > 0
         old = (w[here, :], m[here, :], v[here, :])
         new = adamw_rows(*old, g[0].astype(F32))
         w_out[here, :] = jnp.where(listed, new[0], old[0])
@@ -419,7 +562,7 @@
 def update(where, dl, rows, grad, table, moment_one, moment_two):
     wide = pl.BlockSpec((384, 256), lambda k, s: (0, k))
     grad_spec = [
-        pl.BlockSpec((1, BLOCK, 256), lambda k, s, j=j: (k, s[j], 0)) for j in range(3)
+        pl.BlockSpec((1, BLOCK, 256), lambda k, s, j=j: (k, listed_at(s, j)[0], 0)) for j in range(3)
     ]
     return pl.pallas_call(
         update_kernel,
@@ -442,11 +585,7 @@
 
 def body(tokens, table, moment_one, moment_two, block_ids, targets):
     owner = lax.axis_index(("dp", "vocab"))
-    mine = owner * 3 + jnp.arange(3, dtype=jnp.int32)
-    match = block_ids[None, :] == mine[:, None]
-    listed = jnp.any(match, axis=1).astype(jnp.int32)
-    place = jnp.argmax(match, axis=1).astype(jnp.int32)
-    where = jnp.concatenate([place, listed])
+    where = jnp.concatenate([block_ids, jnp.reshape(owner * 3, (1,)).astype(jnp.int32)])
     rows, dl, grad = communicate(block_ids, tokens, table, targets.reshape(8, 128))
     return tuple(update(where, dl, rows, grad, table, moment_one, moment_two))
 

time: 177 us -> 152 us (0.86)
  Pallas kernels: 172 us -> 149 us
    pallas_call x1, Pallas kernels: 158 us -> 134 us  [communicate(): pl.pallas_call(comm_kernel, out_shape=(jax.ShapeDtypeStruct((8, 1024, 256...]
where the time goes in v2:
time: 152 us
  Pallas kernels  149 us (98%)
  local copies, waits for them, and re-layouts  1.59 us (1%)
    pallas_call x1, Pallas kernels, communicate(): pl.pallas_call(comm_kernel, out_shape=(jax.ShapeDtypeStruct((8, 1024, 256...  134 us
    pallas_call x1, Pallas kernels, update(): pl.pallas_call(update_kernel, grid_spec=pltpu.PrefetchScalarGridSpec(num_...  14.2 us

profile of v2, /device:TPU:1, one launch (start us, length us, event | category | flops | bytes accessed | tf_op | source)
XLA Modules:
  0.0 151.5 jit_solution(17389592092072829532)
XLA Ops:
  0.6 0.7 pad_add_fusion.where_ref
  1.4 0.0 copy-start
  1.4 134.3 %shard_map.93 = (bf16[8,1024,256]{2,1,0:T(8,128)(2,1)}, bf16[1024,1024]{1,0:T(8,128)(2,1)}, bf16[8,1024,256]{2,1,0:T(8,128)(2,1)}) custom-call(s32[8]{0:T(128)} %ids.1, bf16[1024,2048]{1,0:T(8,128)(2,1)} %tokens.1, f32[384,2048]{1,0:T(8,128)} %w.1, s32[8,128]{1,0:T(8,128)} %bitcast.2), custom_call_target="tpu_custom_call" | custom-call | tf_op jit(solution)/shard_map/pallas_call | solution.py:490
  135.7 0.0 copy-done
  135.7 0.0 copy-start.1
  135.7 1.6 %copy-done.1 = bf16[1024,1024]{1,0:T(8,128)(2,1)S(1)} copy-done((bf16[1024,1024]{1,0:T(8,128)(2,1)S(1)}, bf16[1024,1024]{1,0:T(8,128)(2,1)}, u32[]{:S(2)}) %copy-start.1) | copy-done | bytes 2097176
  137.3 14.2 %shard_map.94 = (f32[384,2048]{1,0:T(8,128)}, f32[384,2048]{1,0:T(8,128)}, f32[384,2048]{1,0:T(8,128)}, bf16[1024,2048]{1,0:T(8,128)(2,1)}) custom-call(s32[9]{0:T(128)S(1)} %pad_add_fusion.where_ref, bf16[1024,1024]{1,0:T(8,128)(2,1)S(1)} %copy-done.1, bf16[8,1024,256]{2,1,0:T(8,128)(2,1)} %get-tuple-element.8.rows, ...), custom_call_target="tpu_custom_call" | custom-call | tf_op jit(solution)/shard_map/pallas_call | solution.py:567
Async XLA Ops:
  1.4 134.4 %copy-start = (f32[384,2048]{1,0:T(8,128)S(1)}, f32[384,2048]{1,0:T(8,128)}, u32[]{:S(2)}) copy-start(f32[384,2048]{1,0:T(8,128)} %w.1) | copy-start | bytes 9437188
  135.7 1.6 %copy-start.1 = (bf16[1024,1024]{1,0:T(8,128)(2,1)S(1)}, bf16[1024,1024]{1,0:T(8,128)(2,1)}, u32[]{:S(2)}) copy-start(bf16[1024,1024]{1,0:T(8,128)(2,1)} %get-tuple-element.7.dl) | copy-start | bytes 6291460

commit v3 on v2

--- a/solution.py
+++ b/solution.py
@@ -24,7 +24,9 @@
 decay_rate = 0.1
 epsilon = 1e-08
 
-N_SEM = 289
+RELAYED = 2
+N_SEND = 25
+N_RECV = 181
 
 
 def adamw_rows(weights, first, second, grads):
@@ -32,8 +34,9 @@
     second_new = beta_two * second + (1.0 - beta_two) * grads * grads
     correct_one = 1.0 - beta_one**10
     correct_two = 1.0 - beta_two**10
+    squared = second_new * (1.0 / correct_two)
     update = (
-        first_new / correct_one / (jnp.sqrt(second_new / correct_two) + epsilon)
+        first_new * (1.0 / correct_one) / (squared * lax.rsqrt(squared) + epsilon)
         + decay_rate * weights
     )
     return (weights - learn_rate * update, first_new, second_new)
@@ -49,10 +52,10 @@
 
 def comm_kernel(
     ids, tokens, table, targets,
-    rows_out, dl_out, grad_out,
-    tok, tab, tab6, tab_send, rows, part, wire, dl, dl_t, acc, g_send, g_recv, grad,
-    sums, half_sums, rs1, rs2, rt1, rt2, y1, y2, column,
-    send_sem, recv_sem, local_sem,
+    tok_out, grad_out,
+    tok, target, tab6, tab_send, rows, part, wire, dl, dl_t, acc, g_recv, grad, picked,
+    sums, half_sums, rs1, rs2, rs3, land, y1, y2, column,
+    send_sem, recv_sem, plane_send, local_sem, across_send, across_recv,
 ):
     dp = lax.axis_index("dp")
     z = lax.axis_index("vocab")
@@ -71,14 +74,19 @@
 
     peer = (x * 2 + (1 - c), z, y)
 
+    landed = []
+    phase = []
+
     def send(src, dst, device):
-        i = len(pending)
+        left = plane_send.at[phase[0]] if phase else send_sem.at[len(pending)]
         copy = pltpu.make_async_remote_copy(
-            src_ref=src, dst_ref=dst, send_sem=send_sem.at[i], recv_sem=recv_sem.at[i],
+            src_ref=src, dst_ref=dst, send_sem=left, recv_sem=recv_sem.at[len(landed)],
             device_id=device, device_id_type=MESH,
         )
         copy.start()
-        pending.append(copy)
+        landed.append(copy)
+        if not phase:
+            pending.append(copy)
         return copy
 
     def load(src, dst, i):
@@ -86,11 +94,14 @@
         copy.start()
         return copy
 
-    tab_copy = load(table, tab, 0)
+    tab_copies = [
+        load(table.at[:, k * 256:(k + 1) * 256], acc.at[k, :384, :], 5 + k) for k in range(8)
+    ]
     tok_copy = load(tokens, tok, 1)
+    targets_copy = load(targets, target, 0)
 
     barrier = pltpu.get_barrier_semaphore()
-    partners = [near(a, s) for a in "xzy" for s in (1, -1)] + [peer]
+    partners = [near(a, s) for a in "xzy" for s in (1, -1)] + [near("x", 2), near("z", 2), peer]
     for device in partners:
         pl.semaphore_signal(barrier, inc=1, device_id=device, device_id_type=MESH)
     pl.semaphore_wait(barrier, len(partners))
@@ -149,6 +160,32 @@
                 + self.second[1, h].astype(F32)
             )
 
+    class DirectScatter:
+        def __init__(self, axis, piece, land):
+            self.axis, self.piece, self.land = axis, piece, land
+            self.r = rank[axis]
+            self.sent = []
+
+        def start(self, step):
+            src = self.piece(mod4(self.r + step))
+            self.sent.append(send(src, self.land.at[len(self.sent)], near(self.axis, step)))
+
+        def total(self):
+            for copy in self.sent:
+                copy.wait_recv()
+            value = self.piece(self.r)[...].astype(F32)
+            for i in range(3):
+                value += self.land[i].astype(F32)
+            return value.astype(BF16)
+
+    class DirectGather:
+        def __init__(self, axis, place):
+            own = place(rank[axis])
+            self.sent = {step: send(own, own, near(axis, step)) for step in (1, -1, 2)}
+
+        def arrived(self, step):
+            self.sent[step].wait_recv()
+
     class Gather:
         def __init__(self, axis, place):
             self.axis, self.place = axis, place
@@ -177,7 +214,8 @@
             self.next_up.wait_recv()
             self.next_down.wait_recv()
 
-    def plane_all_reduce(n, result):
+    def plane_all_reduce(n, result, fill):
+        phase.append(n)
         halves = range(2)
         axes = (("x", "z"), ("z", "x"))
 
@@ -189,113 +227,129 @@
         inner = []
         for half, (a, b) in enumerate(axes):
             for i, block in enumerate(blocks_of(half)):
-                def piece(p, h, half=half, block=block):
+                def piece(p, h=None, half=half, block=block):
+                    if h is None:
+                        return sums.at[n, p, rows_at(half * 512 + block * 128, 128), :]
                     return sums.at[n, p, rows_at(half * 512 + block * 128 + h * 64, 64), :]
-                outer[half].append(Scatter(a, piece, rs1.at[n, half, i], rs2.at[n, half, i]))
-            def piece(p, h, half=half):
-                return half_sums.at[n, half, rows_at(p * 128 + h * 64, 64), :]
-            inner.append(Scatter(b, piece, rt1.at[n, half], rt2.at[n, half]))
+                if i < RELAYED:
+                    outer[half].append(Scatter(a, piece, rs1.at[n, half, i], rs2.at[n, half, i]))
+                else:
+                    outer[half].append(DirectScatter(a, piece, rs3.at[n, half, i - RELAYED]))
+            def piece(p, half=half):
+                return half_sums.at[n, half, rows_at(p * 128, 128), :]
+            inner.append(DirectScatter(b, piece, land.at[n, half]))
 
         def finish(half, i):
-            outer[half][i].arrived()
+            one = outer[half][i]
             block = blocks_of(half)[i]
-            for h in range(2):
-                half_sums[n, half, rows_at(block * 128 + h * 64, 64), :] = (
-                    outer[half][i].total(h).astype(BF16)
-                )
-
-        for i in range(4):
+            if i < RELAYED:
+                one.arrived()
+                for h in range(2):
+                    half_sums[n, half, rows_at(block * 128 + h * 64, 64), :] = (
+                        one.total(h).astype(BF16)
+                    )
+            else:
+                half_sums[n, half, rows_at(block * 128, 128), :] = one.total()
+
+        for i in range(RELAYED):
             for half in halves:
                 outer[half][i].far()
             if i >= 1:
                 for half in halves:
                     outer[half][i - 1].direct()
         for half in halves:
-            outer[half][3].direct()
+            outer[half][RELAYED - 1].direct()
+        for i in range(RELAYED, 4):
+            for step in (2, 1, -1):
+                for half in halves:
+                    outer[half][i].start(step)
+        fill()
         for half in halves:
             outer[half][0].relay()
+        fill()
         for half in halves:
             outer[half][1].relay()
-        for half in halves:
-            finish(half, 0)
-            inner[half].far()
-        for half in halves:
-            outer[half][2].relay()
-        for half in halves:
-            finish(half, 1)
-            inner[half].direct_up()
-        for half in halves:
-            outer[half][3].relay()
-        for half in halves:
-            inner[half].relay_up()
-            finish(half, 2)
-            inner[half].direct_down()
-            inner[half].relay_down()
+        for i, step in enumerate((2, 1, -1)):
+            for half in halves:
+                finish(half, i)
+                inner[half].start(step)
+            if i < 2:
+                fill()
         for half in halves:
             finish(half, 3)
 
-        across = []
         inner_gather = []
         outer_gather = [[], []]
 
         def hand_over(half, p, block):
-            ref = result.at[c * 4 + p, rows_at(half * 512 + block * 128, 128), :]
-            across.append(send(ref, ref, peer))
+            ref = result.at[c * 4 + p, half * 4 + block]
+            pltpu.make_async_remote_copy(
+                src_ref=ref, dst_ref=ref, send_sem=across_send.at[n], recv_sem=across_recv.at[n],
+                device_id=peer, device_id_type=MESH,
+            ).start()
 
         def spread(half, block):
             a = axes[half][0]
-            def place(p, h):
+            def place(p, h=None):
                 if h is None:
-                    return result.at[c * 4 + p, rows_at(half * 512 + block * 128, 128), :]
-                return result.at[c * 4 + p, rows_at(half * 512 + block * 128 + h * 64, 64), :]
-            g = Gather(a, place)
-            g.start()
+                    return result.at[c * 4 + p, half * 4 + block]
+                return result.at[c * 4 + p, half * 4 + block, pl.ds(h * 64, 64), :]
+            if len(outer_gather[half]) < 3:
+                g = Gather(a, place)
+                g.start()
+            else:
+                g = DirectGather(a, place)
             outer_gather[half].append((g, block))
             hand_over(half, rank[a], block)
 
         for half, (a, b) in enumerate(axes):
             chunk = c * 4 + rank[a]
-            inner[half].arrived()
-            for h in range(2):
-                result[chunk, rows_at(half * 512 + rank[b] * 128 + h * 64, 64), :] = (
-                    inner[half].total(h).astype(BF16)
-                )
-            def place(p, h, half=half, chunk=chunk):
-                if h is None:
-                    return result.at[chunk, rows_at(half * 512 + p * 128, 128), :]
-                return result.at[chunk, rows_at(half * 512 + p * 128 + h * 64, 64), :]
-            g = Gather(b, place)
-            g.start()
-            inner_gather.append(g)
+            result[chunk, half * 4 + rank[b]] = inner[half].total()
+            def place(p, half=half, chunk=chunk):
+                return result.at[chunk, half * 4 + p]
+            inner_gather.append(DirectGather(b, place))
             spread(half, rank[b])
 
         def spread_relay(half, i):
             g, block = outer_gather[half][i]
-            g.relay_up()
-            hand_over(half, mod4(g.r - 1), block)
-            g.relay_down()
-            hand_over(half, mod4(g.r + 1), block)
+            r = rank[axes[half][0]]
+            if i < 3:
+                g.relay_up()
+            else:
+                g.arrived(1)
+            hand_over(half, mod4(r - 1), block)
+            if i < 3:
+                g.relay_down()
+            else:
+                g.arrived(-1)
+            hand_over(half, mod4(r + 1), block)
 
         def spread_finish(half, i):
             g, block = outer_gather[half][i]
-            g.finish()
-            hand_over(half, mod4(g.r + 2), block)
-
-        for half in halves:
-            g = inner_gather[half]
-            g.relay_up()
-            spread(half, mod4(g.r - 1))
-            g.relay_down()
-            spread(half, mod4(g.r + 1))
+            if i < 3:
+                g.finish()
+            else:
+                g.arrived(2)
+            hand_over(half, mod4(rank[axes[half][0]] + 2), block)
+
+        for half in halves:
+            r = rank[axes[half][1]]
+            inner_gather[half].arrived(1)
+            spread(half, mod4(r - 1))
+            inner_gather[half].arrived(-1)
+            spread(half, mod4(r + 1))
+        fill()
         for half in halves:
             spread_relay(half, 0)
-        for half in halves:
-            g = inner_gather[half]
-            g.finish()
-            spread(half, mod4(g.r + 2))
+        fill()
+        for half in halves:
+            inner_gather[half].arrived(2)
+            spread(half, mod4(rank[axes[half][1]] + 2))
+        fill()
         for half in halves:
             spread_relay(half, 1)
             spread_relay(half, 2)
+        fill()
         for half in halves:
             spread_finish(half, 0)
         for half in halves:
@@ -303,19 +357,29 @@
         for half in halves:
             for i in range(1, 4):
                 spread_finish(half, i)
-        for copy in across:
-            copy.wait_recv()
-
-    tab_copy.wait()
+        across = pltpu.make_async_remote_copy(
+            src_ref=result.at[pl.ds(c * 4, 4)], dst_ref=result.at[pl.ds((1 - c) * 4, 4)],
+            send_sem=across_send.at[n], recv_sem=across_recv.at[n],
+            device_id=peer, device_id_type=MESH,
+        )
+        across.wait_send()
+        across.wait_recv()
+        bytes_sent = tok.at[pl.ds(0, 960), :]
+        pltpu.make_async_remote_copy(
+            src_ref=bytes_sent, dst_ref=bytes_sent, send_sem=plane_send.at[n],
+            recv_sem=plane_send.at[n], device_id=peer, device_id_type=MESH,
+        ).wait_send()
+        phase.pop()
+
+    for copy in tab_copies:
+        copy.wait()
     for k in range(4):
-        cols = pl.ds(pl.multiple_of((1 - c) * 1024 + k * 256, 256), 256)
         for j in range(3):
-            tab_send[j, k] = tab[j * BLOCK:(j + 1) * BLOCK, cols].astype(BF16)
+            tab_send[j, k] = acc[(1 - c) * 4 + k, j * BLOCK:(j + 1) * BLOCK, :].astype(BF16)
     table_half = send(tab_send, tab6.at[pl.ds(c * 3, 3)], peer)
     for k in range(4):
-        cols = pl.ds(pl.multiple_of(c * 1024 + k * 256, 256), 256)
         for j in range(3):
-            tab6[c * 3 + j, k] = tab[j * BLOCK:(j + 1) * BLOCK, cols].astype(BF16)
+            tab6[c * 3 + j, k] = acc[c * 4 + k, j * BLOCK:(j + 1) * BLOCK, :].astype(BF16)
     table_half.wait_recv()
     for b in range(8):
         block = ids[b]
@@ -327,10 +391,10 @@
             sums[0, k, b * BLOCK:(b + 1) * BLOCK, :] = jnp.where(
                 here, tab6[slot, k].astype(F32), 0.0
             ).astype(BF16)
-    plane_all_reduce(0, rows)
-    rows_copy = load(rows, rows_out, 2)
+    plane_all_reduce(0, rows, lambda: None)
 
     tok_copy.wait()
+    targets_copy.wait()
 
     def logits_of(p):
         @pl.loop(0, 4)
@@ -339,7 +403,7 @@
             for k in range(8):
                 total += lax.dot_general(
                     tok[rows_at(p * 256, 256), k * 256:(k + 1) * 256],
-                    rows[k, rows_at(n * 256, 256), :],
+                    rows[k, pl.ds(n * 2, 2)].reshape(256, 256),
                     (((1,), (1,)), ((), ())),
                     preferred_element_type=F32,
                 )
@@ -394,7 +458,7 @@
     gathers = []
     for u in range(2):
         parts[u].arrived()
-        line = targets[pl.ds(y * 2 + u, 1), :].astype(F32)
+        line = target[pl.ds(y * 2 + u, 1), :].astype(F32)
         column[...] = jnp.transpose(jnp.broadcast_to(line, (128, 128)))
 
         @pl.loop(0, 4)
@@ -455,9 +519,9 @@
     each_tile(second)
     for g in gathers:
         g.finish()
-    dl_copy = load(dl, dl_out, 3)
     turn(far)
 
+    g_send = sums.at[0]
     crossing = []
     for q in range(4):
         k = (1 - c) * 4 + q
@@ -474,14 +538,34 @@
             here = rows_at(n * 512, 512)
             total = (acc[k, here, :] + product(far, k, n)) * SCALE
             sums[1, q, here, :] = (total + g_recv[q, here, :].astype(F32)).astype(BF16)
-    plane_all_reduce(1, grad)
-    grad_copy = load(grad, grad_out, 4)
-
-    assert len(pending) == N_SEM, len(pending)
+    chunks = iter(range(8))
+
+    def token_chunk():
+        k = next(chunks)
+
+        @pl.loop(0, 2)
+        def _(n):
+            here = rows_at(n * 512, 512)
+            tok[here, k * 256:(k + 1) * 256] = (
+                jnp.dot(dl[here, :], rows[k].reshape(1024, 256), preferred_element_type=F32) * SCALE
+            ).astype(BF16)
+
+    plane_all_reduce(1, grad, token_chunk)
+    assert next(chunks, None) is None
+    tok_out_copy = load(tok, tok_out, 2)
+    for j in range(3):
+        place = 0
+        for b in range(8):
+            place += b * (ids[b] == (dp * 4 + z) * 3 + j).astype(jnp.int32)
+        place = jnp.minimum(place, 7)
+        for k in range(8):
+            picked[j * BLOCK:(j + 1) * BLOCK, k * 256:(k + 1) * 256] = grad[k, place]
+    grad_copy = load(picked, grad_out, 3)
+
+    assert (len(pending), len(landed)) == (N_SEND, N_RECV), (len(pending), len(landed))
     for copy in pending:
         copy.wait_send()
-    rows_copy.wait()
-    dl_copy.wait()
+    tok_out_copy.wait()
     grad_copy.wait()
 
 
@@ -490,104 +574,85 @@
     return pl.pallas_call(
         comm_kernel,
         out_shape=(
-            jax.ShapeDtypeStruct((8, 1024, 256), BF16),
-            jax.ShapeDtypeStruct((1024, 1024), BF16),
-            jax.ShapeDtypeStruct((8, 1024, 256), BF16),
+            jax.ShapeDtypeStruct((1024, 2048), BF16),
+            jax.ShapeDtypeStruct((384, 2048), BF16),
         ),
         in_specs=[
             pl.BlockSpec(memory_space=pltpu.SMEM),
-            pl.BlockSpec(memory_space=pl.ANY),
-            pl.BlockSpec(memory_space=pl.ANY),
-            pl.BlockSpec(memory_space=pltpu.VMEM),
+            pl.BlockSpec(memory_space=pltpu.HBM),
+            pl.BlockSpec(memory_space=pltpu.HBM),
+            pl.BlockSpec(memory_space=pltpu.HBM),
         ],
-        out_specs=(pl.BlockSpec(memory_space=pl.ANY),) * 3,
+        out_specs=(pl.BlockSpec(memory_space=pl.ANY),) * 2,
         scratch_shapes=[
             vmem((1024, 2048), BF16),
-            vmem((384, 2048), F32),
+            vmem((8, 128), jnp.int32),
             vmem((6, 4, 128, 256), BF16),
             vmem((3, 4, 128, 256), BF16),
-            vmem((8, 1024, 256), BF16),
+            vmem((8, 8, 128, 256), BF16),
             vmem((1024, 1024), F32),
             vmem((1024, 1152), WIRE),
             vmem((1024, 1024), BF16),
             vmem((4, 1024, 256), BF16),
             vmem((8, 1024, 256), F32),
             vmem((4, 1024, 256), BF16),
-            vmem((4, 1024, 256), BF16),
-            vmem((8, 1024, 256), BF16),
+            vmem((8, 8, 128, 256), BF16),
+            vmem((384, 2048), BF16),
             vmem((2, 4, 1024, 256), BF16),
             vmem((2, 2, 512, 256), BF16),
-            vmem((2, 2, 4, 2, 64, 256), BF16),
-            vmem((2, 2, 4, 2, 2, 64, 256), BF16),
-            vmem((2, 2, 2, 64, 256), BF16),
-            vmem((2, 2, 2, 2, 64, 256), BF16),
+            vmem((2, 2, RELAYED, 2, 64, 256), BF16),
+            vmem((2, 2, RELAYED, 2, 2, 64, 256), BF16),
+            vmem((2, 2, 4 - RELAYED, 3, 128, 256), BF16),
+            vmem((2, 2, 3, 128, 256), BF16),
             vmem((2, 2, 64, 1152), WIRE),
             vmem((2, 2, 2, 64, 1152), WIRE),
             vmem((128, 128), F32),
-            pltpu.SemaphoreType.DMA((N_SEM,)),
-            pltpu.SemaphoreType.DMA((N_SEM,)),
-            pltpu.SemaphoreType.DMA((5,)),
+            pltpu.SemaphoreType.DMA((N_SEND,)),
+            pltpu.SemaphoreType.DMA((N_RECV,)),
+            pltpu.SemaphoreType.DMA((2,)),
+            pltpu.SemaphoreType.DMA((13,)),
+            pltpu.SemaphoreType.DMA((2,)),
+            pltpu.SemaphoreType.DMA((2,)),
         ],
         compiler_params=pltpu.CompilerParams(
-            collective_id=0, has_side_effects=True, vmem_limit_bytes=60 * 2**20
+            collective_id=0, has_side_effects=True, vmem_limit_bytes=56 * 2**20
         ),
     )(ids, tokens, table, targets)
 
 
-def listed_at(where, j):
-    place, listed = 0, 0
-    for b in range(8):
-        same = where[b] == where[8] + j
-        place = jnp.where(same, b, place)
-        listed = jnp.where(same, 1, listed)
-    return place, listed
-
-
-def update_kernel(
-    where_ref, dl, rows, g0, g1, g2, w, m, v, w_out, m_out, v_out, tok_out
-):
-    tok_out[...] = (
-        jnp.dot(dl[...], rows[0], preferred_element_type=F32) * SCALE
-    ).astype(BF16)
-    for j, g in enumerate((g0, g1, g2)):
+def update_kernel(where, grad, w, m, v, tok_in, w_out, m_out, v_out, tok_out):
+    tok_out[...] = tok_in[...]
+    for j in range(3):
         here = slice(j * BLOCK, (j + 1) * BLOCK)
-        listed = listed_at(where_ref, j)[1] > 0
+        listed = where[0] == where[8] + j
+        for b in range(1, 8):
+            listed = jnp.logical_or(listed, where[b] == where[8] + j)
         old = (w[here, :], m[here, :], v[here, :])
-        new = adamw_rows(*old, g[0].astype(F32))
+        new = adamw_rows(*old, grad[here, :].astype(F32))
         w_out[here, :] = jnp.where(listed, new[0], old[0])
         m_out[here, :] = jnp.where(listed, new[1], old[1])
         v_out[here, :] = jnp.where(listed, new[2], old[2])
 
 
-def update(where, dl, rows, grad, table, moment_one, moment_two):
-    wide = pl.BlockSpec((384, 256), lambda k, s: (0, k))
-    grad_spec = [
-        pl.BlockSpec((1, BLOCK, 256), lambda k, s, j=j: (k, listed_at(s, j)[0], 0)) for j in range(3)
-    ]
+def update(where, grad, table, moment_one, moment_two, token_grads):
+    wide = pl.BlockSpec((384, 256), lambda k: (0, k))
+    tall = pl.BlockSpec((1024, 256), lambda k: (0, k))
     return pl.pallas_call(
         update_kernel,
-        grid_spec=pltpu.PrefetchScalarGridSpec(
-            num_scalar_prefetch=1,
-            grid=(8,),
-            in_specs=[
-                pl.BlockSpec((1024, 1024), lambda k, s: (0, 0)),
-                pl.BlockSpec((1, 1024, 256), lambda k, s: (k, 0, 0)),
-                *grad_spec,
-                wide, wide, wide,
-            ],
-            out_specs=[wide, wide, wide, pl.BlockSpec((1024, 256), lambda k, s: (0, k))],
-        ),
+        grid=(8,),
+        in_specs=[pl.BlockSpec(memory_space=pltpu.SMEM), wide, wide, wide, wide, tall],
+        out_specs=[wide, wide, wide, tall],
         out_shape=[jax.ShapeDtypeStruct((384, 2048), F32)] * 3
         + [jax.ShapeDtypeStruct((1024, 2048), BF16)],
-        compiler_params=pltpu.CompilerParams(vmem_limit_bytes=48 * 2**20),
-    )(where, dl, rows, grad, grad, grad, table, moment_one, moment_two)
+        compiler_params=pltpu.CompilerParams(vmem_limit_bytes=47 * 2**20),
+    )(where, grad, table, moment_one, moment_two, token_grads)
 
 
 def body(tokens, table, moment_one, moment_two, block_ids, targets):
     owner = lax.axis_index(("dp", "vocab"))
     where = jnp.concatenate([block_ids, jnp.reshape(owner * 3, (1,)).astype(jnp.int32)])
-    rows, dl, grad = communicate(block_ids, tokens, table, targets.reshape(8, 128))
-    return tuple(update(where, dl, rows, grad, table, moment_one, moment_two))
+    token_grads, grad = communicate(where, tokens, table, targets.reshape(8, 128))
+    return tuple(update(where, grad, table, moment_one, moment_two, token_grads))
 
 
 def solution(mesh):

time: 152 us -> 146 us (0.961)
  Pallas kernels: 149 us -> 142 us
    pallas_call x2, Pallas kernels: 149 us -> 142 us  [the longest x1 131 us: communicate(): pl.pallas_call(comm_kernel, out_shape=(jax.ShapeDtypeStruct((1024, 2048),...]
where the time goes in v3:
time: 146 us
  Pallas kernels  142 us (97%)
    pallas_call x1, Pallas kernels, communicate(): pl.pallas_call(comm_kernel, out_shape=(jax.ShapeDtypeStruct((1024, 2048),...  131 us
    pallas_call x1, Pallas kernels, update(): pl.pallas_call(update_kernel, grid=(8,), in_specs=[pl.BlockSpec(memory_sp...  11.3 us

profile of v3, /device:TPU:1, one launch (start us, length us, event | category | flops | bytes accessed | tf_op | source)
XLA Modules:
  0.0 145.6 jit_solution(12319274530011772965)
XLA Ops:
  0.6 1.2 pad_add_fusion.ids.where
  1.9 0.0 copy-start
  1.9 0.0 copy-start.2
  1.9 131.0 %shard_map.93 = (bf16[1024,2048]{1,0:T(8,128)(2,1)}, bf16[384,2048]{1,0:T(8,128)(2,1)}) custom-call(s32[9]{0:T(128)} %pad_add_fusion.ids.where, bf16[1024,2048]{1,0:T(8,128)(2,1)} %tokens.1, f32[384,2048]{1,0:T(8,128)} %w.1, s32[8,128]{1,0:T(8,128)} %bitcast.2), custom_call_target="tpu_custom_call" | custom-call | tf_op jit(solution)/shard_map/pallas_call | solution.py:574
  132.9 0.0 copy-done
  132.9 0.0 copy-done.2
  132.9 0.0 copy-start.1
  132.9 1.4 copy-done.1
  134.3 11.3 %shard_map.94 = (f32[384,2048]{1,0:T(8,128)}, f32[384,2048]{1,0:T(8,128)}, f32[384,2048]{1,0:T(8,128)}, bf16[1024,2048]{1,0:T(8,128)(2,1)}) custom-call(s32[9]{0:T(128)S(1)} %copy-done.2, bf16[384,2048]{1,0:T(8,128)(2,1)S(1)} %copy-done.1, f32[384,2048]{1,0:T(8,128)S(1)} %copy-done, f32[384,2048]{1,0:T(8,128)} %m.1, f32[384,2048]{1,0:T(8,128)} %v.1, ...), custom_call_target="tpu_custom_call" | custom-call | tf_op jit(solution)/shard_map/pallas_call | solution.py:640
Async XLA Ops:
  1.9 131.0 %copy-start = (f32[384,2048]{1,0:T(8,128)S(1)}, f32[384,2048]{1,0:T(8,128)}, u32[]{:S(2)}) copy-start(f32[384,2048]{1,0:T(8,128)} %w.1) | copy-start | bytes 9437188
  1.9 131.0 %copy-start.2 = (s32[9]{0:T(128)S(1)}, s32[9]{0:T(128)}, u32[]{:S(2)}) copy-start(s32[9]{0:T(128)} %pad_add_fusion.ids.where) | copy-start | bytes 112
  132.9 1.4 copy-start.1

commit v4 on v3

--- a/solution.py
+++ b/solution.py
@@ -25,6 +25,7 @@
 epsilon = 1e-08
 
 RELAYED = 2
+STEPS_UPDATE = 4
 N_SEND = 25
 N_RECV = 181
 
@@ -104,6 +105,15 @@
     partners = [near(a, s) for a in "xzy" for s in (1, -1)] + [near("x", 2), near("z", 2), peer]
     for device in partners:
         pl.semaphore_signal(barrier, inc=1, device_id=device, device_id_type=MESH)
+
+    for copy in tab_copies:
+        copy.wait()
+    for k in range(4):
+        for j in range(3):
+            tab_send[j, k] = acc[(1 - c) * 4 + k, j * BLOCK:(j + 1) * BLOCK, :].astype(BF16)
+    for k in range(4):
+        for j in range(3):
+            tab6[c * 3 + j, k] = acc[c * 4 + k, j * BLOCK:(j + 1) * BLOCK, :].astype(BF16)
     pl.semaphore_wait(barrier, len(partners))
 
     class Scatter:
@@ -371,15 +381,7 @@
         ).wait_send()
         phase.pop()
 
-    for copy in tab_copies:
-        copy.wait()
-    for k in range(4):
-        for j in range(3):
-            tab_send[j, k] = acc[(1 - c) * 4 + k, j * BLOCK:(j + 1) * BLOCK, :].astype(BF16)
     table_half = send(tab_send, tab6.at[pl.ds(c * 3, 3)], peer)
-    for k in range(4):
-        for j in range(3):
-            tab6[c * 3 + j, k] = acc[c * 4 + k, j * BLOCK:(j + 1) * BLOCK, :].astype(BF16)
     table_half.wait_recv()
     for b in range(8):
         block = ids[b]
@@ -620,13 +622,16 @@
     )(ids, tokens, table, targets)
 
 
-def update_kernel(where, grad, w, m, v, tok_in, w_out, m_out, v_out, tok_out):
+def update_kernel(ids, grad, w, m, v, tok_in, w_out, m_out, v_out, tok_out):
+    mine = (lax.axis_index('dp') * 4 + lax.axis_index('vocab')) * 3
+    size = w.shape[0] // 3
     tok_out[...] = tok_in[...]
-    for j in range(3):
-        here = slice(j * BLOCK, (j + 1) * BLOCK)
-        listed = where[0] == where[8] + j
+    for part in range(3):
+        here = slice(part * size, (part + 1) * size)
+        block = mine + (pl.program_id(0) * 3 * size + part * size) // BLOCK
+        listed = ids[0] == block
         for b in range(1, 8):
-            listed = jnp.logical_or(listed, where[b] == where[8] + j)
+            listed = jnp.logical_or(listed, ids[b] == block)
         old = (w[here, :], m[here, :], v[here, :])
         new = adamw_rows(*old, grad[here, :].astype(F32))
         w_out[here, :] = jnp.where(listed, new[0], old[0])
@@ -634,25 +639,23 @@
         v_out[here, :] = jnp.where(listed, new[2], old[2])
 
 
-def update(where, grad, table, moment_one, moment_two, token_grads):
-    wide = pl.BlockSpec((384, 256), lambda k: (0, k))
-    tall = pl.BlockSpec((1024, 256), lambda k: (0, k))
+def update(ids, grad, table, moment_one, moment_two, token_grads):
+    wide = pl.BlockSpec((384 // STEPS_UPDATE, 2048), lambda k: (k, 0))
+    tall = pl.BlockSpec((1024 // STEPS_UPDATE, 2048), lambda k: (k, 0))
     return pl.pallas_call(
         update_kernel,
-        grid=(8,),
+        grid=(STEPS_UPDATE,),
         in_specs=[pl.BlockSpec(memory_space=pltpu.SMEM), wide, wide, wide, wide, tall],
         out_specs=[wide, wide, wide, tall],
         out_shape=[jax.ShapeDtypeStruct((384, 2048), F32)] * 3
         + [jax.ShapeDtypeStruct((1024, 2048), BF16)],
         compiler_params=pltpu.CompilerParams(vmem_limit_bytes=47 * 2**20),
-    )(where, grad, table, moment_one, moment_two, token_grads)
+    )(ids, grad, table, moment_one, moment_two, token_grads)
 
 
 def body(tokens, table, moment_one, moment_two, block_ids, targets):
-    owner = lax.axis_index(("dp", "vocab"))
-    where = jnp.concatenate([block_ids, jnp.reshape(owner * 3, (1,)).astype(jnp.int32)])
-    token_grads, grad = communicate(where, tokens, table, targets.reshape(8, 128))
-    return tuple(update(where, grad, table, moment_one, moment_two, token_grads))
+    token_grads, grad = communicate(block_ids, tokens, table, targets.reshape(8, 128))
+    return tuple(update(block_ids, grad, table, moment_one, moment_two, token_grads))
 
 
 def solution(mesh):

time: 146 us -> 142 us (0.973)
  Pallas kernels: 142 us -> 140 us
    pallas_call x1, Pallas kernels: 11.3 us -> 9.27 us  [update(): pl.pallas_call(update_kernel, grid=(STEPS_UPDATE,), in_specs=[pl.BlockSpe...]
where the time goes in v4:
time: 142 us
  Pallas kernels  140 us (99%)
    pallas_call x1, Pallas kernels, communicate(): pl.pallas_call(comm_kernel, out_shape=(jax.ShapeDtypeStruct((1024, 2048),...  131 us
    pallas_call x1, Pallas kernels, update(): pl.pallas_call(update_kernel, grid=(STEPS_UPDATE,), in_specs=[pl.BlockSpe...  9.27 us

profile of v4, /device:TPU:1, one launch (start us, length us, event | category | flops | bytes accessed | tf_op | source)
XLA Modules:
  0.0 142.1 jit_solution(15534352421329549443)
XLA Ops:
  0.6 0.0 copy-start
  0.6 0.0 copy-start.2
  0.7 130.8 %shard_map.93 = (bf16[1024,2048]{1,0:T(8,128)(2,1)}, bf16[384,2048]{1,0:T(8,128)(2,1)}) custom-call(s32[8]{0:T(128)} %ids.3, bf16[1024,2048]{1,0:T(8,128)(2,1)} %tokens.1, f32[384,2048]{1,0:T(8,128)} %w.1, s32[8,128]{1,0:T(8,128)} %bitcast.1), custom_call_target="tpu_custom_call" | custom-call | tf_op jit(solution)/shard_map/pallas_call | solution.py:576
  131.4 0.0 copy-done
  131.4 0.0 copy-done.2
  131.5 0.0 copy-start.1
  131.5 1.4 copy-done.1
  132.9 9.3 %shard_map.94 = (f32[384,2048]{1,0:T(8,128)}, f32[384,2048]{1,0:T(8,128)}, f32[384,2048]{1,0:T(8,128)}, bf16[1024,2048]{1,0:T(8,128)(2,1)}) custom-call(s32[8]{0:T(128)S(1)} %copy-done.2, bf16[384,2048]{1,0:T(8,128)(2,1)S(1)} %copy-done.1, f32[384,2048]{1,0:T(8,128)S(1)} %copy-done, f32[384,2048]{1,0:T(8,128)} %m.1, f32[384,2048]{1,0:T(8,128)} %v.1, ...), custom_call_target="tpu_custom_call" | custom-call | tf_op jit(solution)/shard_map/pallas_call | solution.py:645
Async XLA Ops:
  0.6 130.8 %copy-start = (f32[384,2048]{1,0:T(8,128)S(1)}, f32[384,2048]{1,0:T(8,128)}, u32[]{:S(2)}) copy-start(f32[384,2048]{1,0:T(8,128)} %w.1) | copy-start | bytes 9437188
  0.6 130.8 %copy-start.2 = (s32[8]{0:T(128)S(1)}, s32[8]{0:T(128)}, u32[]{:S(2)}) copy-start(s32[8]{0:T(128)} %ids.3) | copy-start | bytes 100
  131.5 1.4 copy-start.1

commit v5 on v4

--- a/solution.py
+++ b/solution.py
@@ -273,18 +273,17 @@
             for step in (2, 1, -1):
                 for half in halves:
                     outer[half][i].start(step)
-        fill()
+        for _ in range(3):
+            fill()
         for half in halves:
             outer[half][0].relay()
-        fill()
         for half in halves:
             outer[half][1].relay()
         for i, step in enumerate((2, 1, -1)):
             for half in halves:
                 finish(half, i)
                 inner[half].start(step)
-            if i < 2:
-                fill()
+        fill()
         for half in halves:
             finish(half, 3)
 
@@ -342,20 +341,19 @@
                 g.arrived(2)
             hand_over(half, mod4(rank[axes[half][0]] + 2), block)
 
+        for _ in range(3):
+            fill()
         for half in halves:
             r = rank[axes[half][1]]
             inner_gather[half].arrived(1)
             spread(half, mod4(r - 1))
             inner_gather[half].arrived(-1)
             spread(half, mod4(r + 1))
-        fill()
         for half in halves:
             spread_relay(half, 0)
-        fill()
         for half in halves:
             inner_gather[half].arrived(2)
             spread(half, mod4(rank[axes[half][1]] + 2))
-        fill()
         for half in halves:
             spread_relay(half, 1)
             spread_relay(half, 2)
@@ -398,18 +396,18 @@
     tok_copy.wait()
     targets_copy.wait()
 
-    def logits_of(p):
+    def logits_of(start, size):
         @pl.loop(0, 4)
         def _(n):
-            total = jnp.zeros((256, 256), F32)
+            total = jnp.zeros((size, 256), F32)
             for k in range(8):
                 total += lax.dot_general(
-                    tok[rows_at(p * 256, 256), k * 256:(k + 1) * 256],
+                    tok[rows_at(start, size), k * 256:(k + 1) * 256],
                     rows[k, pl.ds(n * 2, 2)].reshape(256, 256),
                     (((1,), (1,)), ((), ())),
                     preferred_element_type=F32,
                 )
-            part[rows_at(p * 256, 256), pl.ds(pl.multiple_of(n * 256, 256), 256)] = total * SCALE
+            part[rows_at(start, size), pl.ds(pl.multiple_of(n * 256, 256), 256)] = total * SCALE
 
     def encode(start):
         @pl.loop(0, 4)
@@ -445,16 +443,16 @@
             return self.encoded(p, h)
 
     parts = [LogitScatter(u) for u in range(2)]
-    logits_of(mod4(y + 2))
-    parts[0].far()
-    parts[1].far()
-    logits_of(mod4(y + 1))
+    for u in range(2):
+        logits_of(mod4(y + 2) * 256 + u * 128, 128)
+        parts[u].far()
+    logits_of(mod4(y + 1) * 256, 256)
     parts[0].direct_up()
-    logits_of(mod4(y - 1))
+    logits_of(mod4(y - 1) * 256, 256)
     parts[0].direct_down()
     parts[0].relay()
     parts[1].direct()
-    logits_of(y)
+    logits_of(y * 256, 256)
     parts[1].relay()
 
     gathers = []

time: 142 us -> 141 us (level)
  no operation moved by 1% of the time
where the time goes in v5:
time: 141 us
  Pallas kernels  139 us (99%)
  local copies, waits for them, and re-layouts  1.41 us (1%)
    pallas_call x1, Pallas kernels, communicate(): pl.pallas_call(comm_kernel, out_shape=(jax.ShapeDtypeStruct((1024, 2048),...  130 us
    pallas_call x1, Pallas kernels, update(): pl.pallas_call(update_kernel, grid=(STEPS_UPDATE,), in_specs=[pl.BlockSpe...  9.27 us

profile of v5, /device:TPU:1, one launch (start us, length us, event | category | flops | bytes accessed | tf_op | source)
XLA Modules:
  0.0 141.0 jit_solution(2319784000683861591)
XLA Ops:
  0.6 0.0 copy-start
  0.6 0.0 copy-start.2
  0.7 129.6 %shard_map.93 = (bf16[1024,2048]{1,0:T(8,128)(2,1)}, bf16[384,2048]{1,0:T(8,128)(2,1)}) custom-call(s32[8]{0:T(128)} %ids.3, bf16[1024,2048]{1,0:T(8,128)(2,1)} %tokens.1, f32[384,2048]{1,0:T(8,128)} %w.1, s32[8,128]{1,0:T(8,128)} %bitcast.1), custom_call_target="tpu_custom_call" | custom-call | tf_op jit(solution)/shard_map/pallas_call | solution.py:574
  130.3 0.0 copy-done
  130.3 0.0 copy-done.2
  130.3 0.0 copy-start.1
  130.3 1.4 copy-done.1
  131.7 9.3 %shard_map.94 = (f32[384,2048]{1,0:T(8,128)}, f32[384,2048]{1,0:T(8,128)}, f32[384,2048]{1,0:T(8,128)}, bf16[1024,2048]{1,0:T(8,128)(2,1)}) custom-call(s32[8]{0:T(128)S(1)} %copy-done.2, bf16[384,2048]{1,0:T(8,128)(2,1)S(1)} %copy-done.1, f32[384,2048]{1,0:T(8,128)S(1)} %copy-done, f32[384,2048]{1,0:T(8,128)} %m.1, f32[384,2048]{1,0:T(8,128)} %v.1, ...), custom_call_target="tpu_custom_call" | custom-call | tf_op jit(solution)/shard_map/pallas_call | solution.py:643
Async XLA Ops:
  0.6 129.6 %copy-start = (f32[384,2048]{1,0:T(8,128)S(1)}, f32[384,2048]{1,0:T(8,128)}, u32[]{:S(2)}) copy-start(f32[384,2048]{1,0:T(8,128)} %w.1) | copy-start | bytes 9437188
  0.6 129.6 %copy-start.2 = (s32[8]{0:T(128)S(1)}, s32[8]{0:T(128)}, u32[]{:S(2)}) copy-start(s32[8]{0:T(128)} %ids.3) | copy-start | bytes 100
  130.3 1.4 copy-start.1

commit v6 on v5

--- a/solution.py
+++ b/solution.py
@@ -25,7 +25,7 @@
 epsilon = 1e-08
 
 RELAYED = 2
-STEPS_UPDATE = 4
+STEPS_UPDATE = 2
 N_SEND = 25
 N_RECV = 181
 

time: 141 us -> 140 us (level)
  no operation moved by 1% of the time
where the time goes in v6:
time: 140 us
  Pallas kernels  138 us (99%)
  local copies, waits for them, and re-layouts  1.41 us (1%)
    pallas_call x1, Pallas kernels, communicate(): pl.pallas_call(comm_kernel, out_shape=(jax.ShapeDtypeStruct((1024, 2048),...  130 us
    pallas_call x1, Pallas kernels, update(): pl.pallas_call(update_kernel, grid=(STEPS_UPDATE,), in_specs=[pl.BlockSpe...  8.27 us

profile of v6, /device:TPU:1, one launch (start us, length us, event | category | flops | bytes accessed | tf_op | source)
XLA Modules:
  0.0 140.0 jit_solution(14057173692985802950)
XLA Ops:
  0.6 0.0 copy-start
  0.6 0.0 copy-start.2
  0.7 129.6 %shard_map.93 = (bf16[1024,2048]{1,0:T(8,128)(2,1)}, bf16[384,2048]{1,0:T(8,128)(2,1)}) custom-call(s32[8]{0:T(128)} %ids.3, bf16[1024,2048]{1,0:T(8,128)(2,1)} %tokens.1, f32[384,2048]{1,0:T(8,128)} %w.1, s32[8,128]{1,0:T(8,128)} %bitcast.1), custom_call_target="tpu_custom_call" | custom-call | tf_op jit(solution)/shard_map/pallas_call | solution.py:574
  130.3 0.0 copy-done
  130.3 0.0 copy-done.2
  130.3 0.0 copy-start.1
  130.3 1.4 copy-done.1
  131.7 8.3 %shard_map.94 = (f32[384,2048]{1,0:T(8,128)}, f32[384,2048]{1,0:T(8,128)}, f32[384,2048]{1,0:T(8,128)}, bf16[1024,2048]{1,0:T(8,128)(2,1)}) custom-call(s32[8]{0:T(128)S(1)} %copy-done.2, bf16[384,2048]{1,0:T(8,128)(2,1)S(1)} %copy-done.1, f32[384,2048]{1,0:T(8,128)S(1)} %copy-done, f32[384,2048]{1,0:T(8,128)} %m.1, f32[384,2048]{1,0:T(8,128)} %v.1, ...), custom_call_target="tpu_custom_call" | custom-call | tf_op jit(solution)/shard_map/pallas_call | solution.py:643
Async XLA Ops:
  0.6 129.6 %copy-start = (f32[384,2048]{1,0:T(8,128)S(1)}, f32[384,2048]{1,0:T(8,128)}, u32[]{:S(2)}) copy-start(f32[384,2048]{1,0:T(8,128)} %w.1) | copy-start | bytes 9437188
  0.6 129.6 %copy-start.2 = (s32[8]{0:T(128)S(1)}, s32[8]{0:T(128)}, u32[]{:S(2)}) copy-start(s32[8]{0:T(128)} %ids.3) | copy-start | bytes 100
  130.3 1.4 %copy-start.1 = (bf16[384,2048]{1,0:T(8,128)(2,1)S(1)}, bf16[384,2048]{1,0:T(8,128)(2,1)}, u32[]{:S(2)}) copy-start(bf16[384,2048]{1,0:T(8,128)(2,1)} %get-tuple-element.6.grad) | copy-start | bytes 4718596
